TPU v7x, 256 devices: a whole 4x4x8 slice. The times are simulated.
256 devices in a mesh: prow: 8 (over x, core), pcol: 32 (over z, y).
Axes of the slice: x: 4, y: 4, z: 8, core: 2. Of those that a mesh axis runs over, the one named last changes fastest.
Arguments:
- trailing: float32 [16384, 16384], P('prow', 'pcol'), may hold values from -8 to 8
- panel: float32 [16384, 128], P(('prow', 'pcol')), may hold values from -3 to 3, as said below
Outputs:
- updated: float32 [16384, 16384], P('prow', 'pcol')
- reflectors: float32 [16384, 128], P('prow')
- factor: float32 [128, 128], replicated
- band_block: float32 [128, 128], replicated
- first_factor: float32 [128, 128], replicated
Inputs may be any that keep to these rules, and one draw needn't show every extreme that they name: `panel`: rows 0 to 127 are twice the identity plus entries between 0 and 0.25.
All inputs are finite; a program needn't handle non-finite values.
Results may differ from a plain program's by a relative error of at most 0.0003.
Values sent between devices are 32-bit elements; how exact they have to be, the bound alone decides.
No kernel may reach another device: no remote copies, remote signals or barrier semaphores. Data moves between devices by JAX's collectives and lax.ppermute only.
A program may use at most 64 MiB of HBM per device.

v0:
```python
import functools

import jax
import jax.numpy as jnp
from jax import lax
from jax.experimental import pallas as pl
from jax.experimental.pallas import tpu as pltpu
from jax.sharding import PartitionSpec as P

HIGHEST = lax.Precision.HIGHEST
ROWS, ZS, YS = 8, 8, 4
PARTS = 4
NN = (((1,), (0,)), ((), ()))
NT = (((1,), (1,)), ((), ()))
TN = (((0,), (0,)), ((), ()))


def dot(left, right, dims=NN, precision=HIGHEST):
    return lax.dot_general(
        left, right, dims, precision=precision, preferred_element_type=jnp.float32
    )


def eliminate(mats):
    n = mats[0].shape[0]
    lane = lax.broadcasted_iota(jnp.int32, (8, n), 1)
    sub = lax.broadcasted_iota(jnp.int32, (8, n), 0)
    across = lambda x, k: jnp.broadcast_to(x[:, k : k + 1], (8, n))
    down = lambda x, s: jnp.broadcast_to(x[s : s + 1], (8, n))
    tiles = [[m[8 * t : 8 * t + 8] for t in range(n // 8)] for m in mats]
    for t in range(n // 8):
        base = 8 * t
        block = (lane >= base) & (lane < base + 8)
        for m in tiles:
            cols = [across(m[t], base + s) for s in range(8)]
            work = m[t]
            invs, rows, heads = [], [], []
            for s in range(8):
                here = lane == base + s
                below = sub > s
                inv = pl.reciprocal(down(cols[s], s), approx=True)
                row = jnp.where(here, 1.0, down(work, s))
                low = jnp.where(below, cols[s], 0.0)
                work = jnp.where(here & below, 0.0, work) - (low * row) * inv
                head = [down(cols[q], s) for q in range(s + 1, 8)]
                for q in range(s + 1, 8):
                    cols[q] = cols[q] - (low * head[q - s - 1]) * inv
                invs.append(inv)
                rows.append(jnp.where(block & (lane > base + s), 0.0, row))
                heads.append(head)
            m[t] = work
            for j in range(t + 1, n // 8):
                cols = [across(m[j], base + s) for s in range(8)]
                new = jnp.where(block, 0.0, m[j])
                for s in range(8):
                    mult = cols[s] * invs[s]
                    new = new - mult * rows[s]
                    for q in range(s + 1, 8):
                        cols[q] = cols[q] - mult * heads[s][q - s - 1]
                m[j] = new
    return [jnp.concatenate(m, 0) for m in tiles]


def positions(n):
    row = lax.broadcasted_iota(jnp.int32, (n, n), 0)
    col = lax.broadcasted_iota(jnp.int32, (n, n), 1)
    return row, col


def cholesky_pair(gram):
    (packed,) = eliminate([gram])
    row, col = positions(gram.shape[0])
    pivots = jnp.sum(jnp.where(row == col, packed, 0.0), 1, keepdims=True)
    scale = 1.0 / jnp.sqrt(pivots)
    upper = jnp.where(col >= row, packed, 0.0) * scale
    inverse = jnp.where(col < row, packed, jnp.where(col == row, 1.0, 0.0)) * scale
    return upper, inverse


def split(x):
    high = x.astype(jnp.bfloat16)
    return high, (x - high.astype(jnp.float32)).astype(jnp.bfloat16)


def dot_split(left, right, dims=NN):
    small = dot(left[1], right[0], dims, None) + dot(left[0], right[1], dims, None)
    return small + dot(left[0], right[0], dims, None)


def four_sum(refs):
    one, two, three, four = (ref[...] for ref in refs)
    return (one + two) + (three + four)


def panel_kernel(place_ref, *refs):
    stacks, (trailing_ref, panel_ref, mine_ref, away_ref, halves_ref) = refs[:YS], refs[YS:]
    rows, cols = trailing_ref.shape
    chunk, width = stacks[0].shape[1:]
    tile = rows // PARTS
    y = place_ref[1] % YS
    for far, stack in enumerate(stacks):
        for z in range(ZS):
            at = (z * YS + (y ^ far)) * chunk
            panel_ref[pl.ds(pl.multiple_of(at, chunk), chunk), :] = stack[z]
    panel = panel_ref[...]
    gram = dot(panel, panel, TN)
    leading = jnp.where(place_ref[0] == 0, panel[:width], 0.0)
    total = jnp.zeros((width, cols), jnp.float32)
    for part in range(PARTS):
        span = slice(part * tile, (part + 1) * tile)
        total = total + dot(panel[span], trailing_ref[span, :], TN)
    total = total.T
    for core in range(2):
        at = core * halves_ref.shape[0] // 2
        for block in (gram, total, leading):
            part = block.shape[0] // 2
            halves_ref[at : at + part, :] = block[core * part : (core + 1) * part]
            at += part
    core = place_ref[0] % 2
    half = halves_ref.shape[0] // 2
    mine_ref[...] = halves_ref[pl.ds(pl.multiple_of(core * half, 8), half), :]
    away_ref[...] = halves_ref[pl.ds(pl.multiple_of((1 - core) * half, 8), half), :]


def first_kernel(place_ref, mine_ref, other_ref, panel_ref, upper_ref, upper_copy_ref, inverse_ref, ortho_ref, gram_ref):
    part = panel_ref.shape[1] // 2
    mine, other = mine_ref[:part, :], other_ref[:part, :]
    first = place_ref[0] % 2 == 0
    gram = jnp.concatenate([jnp.where(first, mine, other), jnp.where(first, other, mine)], 0)
    upper, inverse = cholesky_pair(gram)
    upper_ref[...] = upper
    upper_copy_ref[...] = upper
    inverse_ref[...] = inverse
    ortho = dot(panel_ref[...], inverse, NT)
    ortho_ref[...] = ortho
    gram_ref[...] = dot(ortho, ortho, TN)


def second_kernel(*refs):
    upper_one_ref, inverse_one_ref, leading_ref = refs[4:7]
    inverse_two_ref, band_ref, band_inverse_t_ref, square_ref = refs[7:]
    upper, inverse = cholesky_pair(four_sum(refs[:4]))
    row, col = positions(upper.shape[0])
    inverse_one = inverse_one_ref[...]
    inverse_two_ref[...] = inverse
    band_ref[...] = dot(upper, upper_one_ref[...])
    band_inverse_t_ref[...] = dot(inverse, inverse_one)
    top = dot(dot(leading_ref[...], inverse_one, NT), inverse, NT)
    square_ref[...] = top + jnp.where(row == col, 1.0, 0.0)


def third_kernel(square_ref, factor_ref, upper_inverse_ref, square_inverse_ref):
    square = square_ref[...]
    one, two = eliminate([square, square.T])
    row, col = positions(square.shape[0])
    unit = jnp.where(row == col, 1.0, 0.0)
    pivots = jnp.sum(jnp.where(row == col, two, 0.0), 1, keepdims=True)
    upper = jnp.where(col >= row, one, 0.0)
    lower_inverse = jnp.where(col < row, one, unit)
    upper_inverse = (jnp.where(col < row, two, unit) / pivots).T
    factor_ref[...] = dot(upper, lower_inverse, NT)
    upper_inverse_ref[...] = upper_inverse
    square_inverse_ref[...] = dot(upper_inverse, lower_inverse)


def block_call(body, outs, name, cost, args, **more):
    return pl.pallas_call(
        body,
        out_shape=[jax.ShapeDtypeStruct(shape, jnp.float32) for shape in outs],
        name=name,
        cost_estimate=pl.CostEstimate(flops=cost, bytes_accessed=1 << 20, transcendentals=0),
        compiler_params=pltpu.CompilerParams(vmem_limit_bytes=40 << 20),
        **more,
    )(*args)


def whole(count):
    return [pl.BlockSpec(memory_space=pltpu.VMEM)] * count


def scalars():
    return pl.BlockSpec(memory_space=pltpu.SMEM)


def unit_rows(start, count, width):
    place = start + lax.broadcasted_iota(jnp.int32, (count, width), 0)
    return jnp.where(place == lax.broadcasted_iota(jnp.int32, (count, width), 1), 1.0, 0.0)


def image_kernel(place_ref, *refs):
    products, edges = refs[:YS], refs[YS : YS + 2]
    ortho_ref, inverse_two_ref, band_inverse_t_ref, base_ref, image_ref, weight_ref = refs[YS + 2 :]
    cols, width = products[0].shape
    y = place_ref[1] % YS
    inverse_two = split(inverse_two_ref[...])
    band_inverse_t = band_inverse_t_ref[...]
    weight = jnp.zeros((width, width), jnp.float32)
    for far in range(YS):
        at = pl.multiple_of((y ^ far) * cols, cols)
        span = pl.ds(at, cols)
        start = place_ref[0] * (YS * cols) + at
        base = dot_split(split(ortho_ref[span, :]), inverse_two, NT) + unit_rows(start, cols, width)
        image = dot(products[far][...], band_inverse_t, NT) + edges[far // 2][(far % 2) * cols : (far % 2 + 1) * cols, :]
        base_ref[span, :] = base
        image_ref[span, :] = image
        weight = weight + dot_split(split(base), split(image), TN)
    weight_ref[...] = weight


def left_kernel(place_ref, base_ref, panel_ref, product_ref, edge_ref, inverse_one_ref, inverse_two_ref, band_inverse_t_ref, square_inverse_ref, upper_inverse_ref, left_ref, reflectors_ref, left_cols_ref, image_cols_ref):
    rows, width = base_ref.shape
    cols = panel_ref.shape[0]
    square_inverse = square_inverse_ref[...]
    table = split(jnp.concatenate([square_inverse, upper_inverse_ref[...]], 1))
    both = dot_split(split(base_ref[...]), table)
    left_ref[...] = both[:, :width]
    place = place_ref[0] * rows + lax.broadcasted_iota(jnp.int32, (rows, width), 0)
    lane = lax.broadcasted_iota(jnp.int32, (rows, width), 1)
    reflectors_ref[...] = jnp.where(place < lane, 0.0, jnp.where(place == lane, 1.0, both[:, width:]))
    ortho = dot(panel_ref[...], inverse_one_ref[...], NT)
    base = dot_split(split(ortho), split(inverse_two_ref[...]), NT) + unit_rows(place_ref[1] * cols, cols, width)
    left_cols_ref[...] = dot_split(split(base), split(square_inverse))
    image_cols_ref[...] = dot(product_ref[...], band_inverse_t_ref[...], NT) + edge_ref[...]


def update_kernel(*refs):
    trailing_ref, left_ref, image_ref, left_cols_ref, image_cols_ref, updated_ref, high_ref, low_ref, weight_high_ref, weight_low_ref = refs[4:]

    @pl.when(pl.program_id(0) == 0)
    def _():
        weight_high_ref[...], weight_low_ref[...] = split(0.5 * four_sum(refs[:4]))
        weight = weight_high_ref[...], weight_low_ref[...]
        left = left_cols_ref[...]
        right = image_cols_ref[...] - dot_split(split(left), weight)
        high_ref[...], low_ref[...] = split(jnp.concatenate([right, left], 1))

    left = left_ref[...]
    pieces = split(left)
    right = image_ref[...] - dot_split(pieces, (weight_high_ref[...], weight_low_ref[...]))
    rights = split(right)
    pair = tuple(jnp.concatenate([one, two], 1) for one, two in zip(pieces, rights))
    updated_ref[...] = trailing_ref[...] - dot_split(pair, (high_ref[...], low_ref[...]), NT)


def update(weights, trailing, left, image, left_cols, image_cols, steps=8):
    rows, cols = trailing.shape
    width = left.shape[1]
    tile = rows // steps
    moving = lambda step: (step, 0)
    fixed = lambda step: (0, 0)
    range_spec = pl.BlockSpec((tile, width), moving)
    cols_spec = pl.BlockSpec((cols, width), fixed)
    square_spec = pl.BlockSpec((width, width), fixed)
    tile_spec = pl.BlockSpec((tile, cols), moving)
    return block_call(
        update_kernel,
        [(rows, cols)],
        "update",
        1 << 32,
        [*weights, trailing, left, image, left_cols, image_cols],
        grid=(steps,),
        in_specs=[square_spec] * 4 + [tile_spec] + [range_spec] * 2 + [cols_spec] * 2,
        out_specs=[tile_spec],
        scratch_shapes=[pltpu.VMEM((cols, 2 * width), jnp.bfloat16)] * 2
        + [pltpu.VMEM((width, width), jnp.bfloat16)] * 2,
    )[0]


def swap_row(x, mask):
    return lax.ppermute(x, "prow", [(r, r ^ mask) for r in range(ROWS)])


def swap_y(x, mask):
    return lax.ppermute(x, "pcol", [(c, c ^ mask) for c in range(ZS * YS)])


def turn_z(x):
    pairs = [(r, z, z ^ (r // 2 + 4 * (r % 2))) for r in range(ROWS) for z in range(ZS)]
    return lax.ppermute(x, ("prow", "pcol"), [(place_of(r, z, y), place_of(r, t, y)) for r, z, t in pairs for y in range(YS)])


def turn_row(x, back=False):
    pairs = [(r, z, z ^ (r // 2 + 4 * (r % 2))) for r in range(ROWS) for z in range(ZS)]
    moves = [(place_of(r, z, y), place_of(t, z, y)) for r, z, t in pairs for y in range(YS)]
    if back:
        moves = [(t, f) for f, t in moves]
    return lax.ppermute(x, ("prow", "pcol"), moves)


def place_of(r, z, y):
    return (r * ZS + z) * YS + y


def three_rows(x):
    return [x] + [swap_row(x, 2 * mask) for mask in (1, 2, 3)]


def along_y(x):
    return [x] + [swap_y(x, mask) for mask in range(1, YS)]


def hold(*arrays):
    return lax.optimization_barrier(arrays)


def on_device(trailing, panel):
    rows, cols = trailing.shape
    chunk, width = panel.shape
    square = (width, width)
    row_index = lax.axis_index("prow")
    col_index = lax.axis_index("pcol")
    core = row_index % 2
    y = col_index % YS
    place = jnp.stack([row_index, col_index]).astype(jnp.int32)

    lines = [[z * YS + at for z in range(ZS)] for at in range(YS)]
    copies = jnp.broadcast_to(panel[None], (ZS, chunk, width))
    source, copies = hold(trailing[:width], copies)
    stack = lax.all_to_all(copies, "pcol", 0, 0, axis_index_groups=lines)
    edge = source.T
    pair = lax.ppermute(edge, "prow", [(0, 1)])
    pair = jnp.where(row_index == 0, edge, pair)
    arrived = [
        lax.ppermute(pair, "prow", [(0, 2 * far), (1, 2 * far + 1)]) for far in (1, 2, 3)
    ]
    edge_cols = jnp.where(row_index < 2, pair, arrived[0] + arrived[1] + arrived[2])

    edge_turned = turn_z(edge_cols)
    half = (cols + 2 * width) // 2
    panel_rows, mine, away = block_call(
        panel_kernel,
        [(rows, width), (half, width), (half, width)],
        "panel",
        1 << 32,
        [place] + along_y(stack) + [trailing],
        in_specs=[scalars()] + whole(YS + 1),
        out_specs=whole(3),
        scratch_shapes=[pltpu.VMEM((2 * half, width), jnp.float32)],
    )
    panel_rows, mine, away, edge_turned = hold(panel_rows, mine, away, edge_turned)

    edge_turned = turn_row(edge_turned)
    messages = three_rows(mine + swap_row(away, 1))
    panel_cols = lax.dynamic_slice_in_dim(panel_rows, y * cols, cols, 0)
    panel_cols = turn_row(panel_cols, back=True)
    messages[1], edge_turned, panel_cols = hold(messages[1], edge_turned, panel_cols)
    edge_pair = jnp.concatenate([edge_turned, swap_y(edge_turned, 1)], 0)
    panel_cols = turn_z(panel_cols)

    mine = (messages[0] + messages[1]) + (messages[2] + messages[3])
    mine, other = hold(mine, swap_row(mine, 1))
    summed = jnp.where(
        core == 0, jnp.stack([mine, other], 0), jnp.stack([other, mine], 0)
    )
    product_cols = summed[:, width // 2 : (width + cols) // 2].reshape(cols, width)
    leading = summed[:, (width + cols) // 2 :].reshape(square)
    product_turned = turn_z(product_cols)
    upper_one, upper_copy, inverse_one, ortho_rows, gram = block_call(
        first_kernel,
        [square, square, square, (rows, width), square],
        "first",
        1 << 33,
        [place, mine, other, panel_rows],
        in_specs=[scalars()] + whole(3),
        out_specs=whole(5),
    )
    gram, product_turned, panel_cols, edge_pair = hold(gram, product_turned, panel_cols, edge_pair)

    gram = gram + swap_row(gram, 1)
    product_turned = turn_row(product_turned)
    grams = three_rows(gram)
    *grams, product_turned = hold(*grams, product_turned)

    turned = along_y(product_turned)
    edges = [edge_pair, swap_y(edge_pair, 2)]
    inverse_two, band_block, band_inverse_t, top = block_call(
        second_kernel, [square] * 4, "second", 1 << 33, grams + [upper_copy, inverse_one, leading],
        in_specs=whole(7), out_specs=whole(4),
    )
    factor, upper_inverse, square_inverse = block_call(
        third_kernel, [square] * 3, "third", 1 << 33, [top], in_specs=whole(1), out_specs=whole(3)
    )
    square_inverse, *turned = hold(square_inverse, *turned)
    base, image, weight = block_call(
        image_kernel,
        [(rows, width)] * 2 + [square],
        "image",
        1 << 31,
        [place] + turned + edges + [ortho_rows, inverse_two, band_inverse_t],
        in_specs=[scalars()] + whole(YS + 5),
        out_specs=whole(3),
    )

    weight = weight + swap_row(weight, 1)
    weight, base = hold(weight, base)
    weights = three_rows(weight)
    left, reflectors, left_cols, image_cols = block_call(
        left_kernel,
        [(rows, width)] * 2 + [(cols, width)] * 2,
        "left",
        1 << 31,
        [place, base, panel_cols, product_cols, edge_cols, inverse_one, inverse_two, band_inverse_t, square_inverse, upper_inverse],
        in_specs=[scalars()] + whole(9),
        out_specs=whole(4),
    )
    updated = update(weights, trailing, left, image, left_cols, image_cols)
    return (updated, reflectors, factor, band_block, upper_one)


def solution(mesh):
    placed = (P("prow", "pcol"), P(("prow", "pcol"), None))
    return jax.shard_map(
        on_device,
        mesh=mesh,
        in_specs=placed,
        out_specs=(P("prow", "pcol"), P("prow", None), P(), P(), P()),
        check_vma=False,
    )
```

profile of v0, /device:TPU:64, one launch (start us, length us, event | category | flops | bytes accessed | tf_op | source)
XLA Modules:
  0.0 139.7 jit_solution(17664697385241022476)
XLA Ops:
  0.6 1.0 slice.9
  1.7 1.5 %broadcast_in_dim.2 = f32[8,64,128]{2,1,0:T(8,128)} broadcast(f32[64,128]{1,0:T(8,128)} %param.3), dimensions={1,2} | broadcast | bytes 294912 | tf_op jit(solution)/shard_map/broadcast_in_dim | solution.py:317
  3.2 1.7 %collective-permute-start.3 = (f32[512,128]{1,0:T(8,128)S(1)}, f32[512,128]{1,0:T(8,128)S(1)}, u32[]{:S(2)}, u32[]{:S(2)}) collective-permute-start(f32[512,128]{1,0:T(8,128)S(1)} %bitcast.13), channel_id=1, source_target_pairs={{0,32},{1,33},{2,34},{3,35},{4,36},{5,37},{6,38},{7,39},{8,40},{9,... | collective-permute-start | bytes 786440 | tf_op jit(solution)/shard_map/ppermute | solution.py:321
  5.0 8.1 %all-to-all-start = ((f32[8,64,128]{2,1,0:T(8,128)}), f32[8,64,128]{2,1,0:T(8,128)S(1)}, u32[]{:S(2)}, u32[]{:S(2)}) async-start(f32[8,64,128]{2,1,0:T(8,128)} %broadcast_in_dim.2), calls=%async_computation | async-start | bytes 524288 | tf_op jit(solution)/shard_map/all_to_all | solution.py:319
  13.1 3.6 %collective-permute-start.6 = (f32[512,128]{1,0:T(8,128)S(1)}, f32[512,128]{1,0:T(8,128)S(1)}, u32[]{:S(2)}, u32[]{:S(2)}) collective-permute-start(f32[512,128]{1,0:T(8,128)S(1)} %broadcast_select_fusion), channel_id=1, source_target_pairs={{0,192},{32,224},{1,193},{33,225},{2,194},{34,226},{3,195},{35,227... | collective-permute-start | bytes 786440 | tf_op jit(solution)/shard_map/ppermute | solution.py:324
  16.7 1.3 collective-permute-start.5
  18.1 1.3 collective-permute-start.4
  19.4 2.4 %all-to-all-done.refs_0_ = f32[8,64,128]{2,1,0:T(8,128)S(1)} async-done(((f32[8,64,128]{2,1,0:T(8,128)}), f32[8,64,128]{2,1,0:T(8,128)S(1)}, u32[]{:S(2)}, u32[]{:S(2)}) %all-to-all-start) | async-done | bytes 262176 | tf_op jit(solution)/shard_map/all_to_all | solution.py:319
  21.7 3.0 %collective-permute-start.2 = (f32[8,64,128]{2,1,0:T(8,128)S(1)}, f32[8,64,128]{2,1,0:T(8,128)S(1)}, u32[]{:S(2)}, u32[]{:S(2)}) collective-permute-start(f32[8,64,128]{2,1,0:T(8,128)S(1)} %all-to-all-done.refs_0_), channel_id=1, source_target_pairs={{0,3},{1,2},{2,1},{3,0},{4,7},{5,6},{6,5},{7,4},{8,11},{9,10},{10,... | collective-permute-start | bytes 786440 | tf_op jit(solution)/shard_map/ppermute | solution.py:274
  24.8 0.6 collective-permute-start.1
  25.4 0.5 collective-permute-start
  25.9 2.7 %collective-permute-done.4 = f32[512,128]{1,0:T(8,128)S(1)} collective-permute-done((f32[512,128]{1,0:T(8,128)S(1)}, f32[512,128]{1,0:T(8,128)S(1)}, u32[]{:S(2)}, u32[]{:S(2)}) %collective-permute-start.4) | collective-permute-done | bytes 262176 | tf_op jit(solution)/shard_map/ppermute | solution.py:324
  28.7 0.7 collective-permute-start.7
  29.4 3.7 %collective-permute-done.2.refs_3_ = f32[8,64,128]{2,1,0:T(8,128)S(1)} collective-permute-done((f32[8,64,128]{2,1,0:T(8,128)S(1)}, f32[8,64,128]{2,1,0:T(8,128)S(1)}, u32[]{:S(2)}, u32[]{:S(2)}) %collective-permute-start.2) | collective-permute-done | bytes 262176 | tf_op jit(solution)/shard_map/ppermute | solution.py:274
  33.0 0.9 collective-permute-done.1.refs_2_
  34.0 0.5 collective-permute-done.refs_1_
  34.4 2.2 %copy-done = f32[2048,512]{1,0:T(8,128)S(1)} copy-done((f32[2048,512]{1,0:T(8,128)S(1)}, f32[2048,512]{1,0:T(8,128)}, u32[]{:S(2)}) %copy-start) | copy-done | bytes 4194328
  36.6 3.8 %panel.1 = (f32[2048,128]{1,0:T(8,128)S(1)}, f32[384,128]{1,0:T(8,128)S(1)}, f32[384,128]{1,0:T(8,128)S(1)}) custom-call(s32[2]{0:T(128)S(1)} %pad_add_fusion.place_ref, f32[8,64,128]{2,1,0:T(8,128)S(1)} %all-to-all-done.refs_0_, f32[8,64,128]{2,1,0:T(8,128)S(1)} %collective-permute-done.refs_1_, f32[8,64,128]{2,1,0:T(8,128)S(1)} %collective-permute-done.1.refs_2_, ...), custom_call_target="tpu_custom_call" | custom-call | flops 4294967296 | bytes 1048576 | tf_op jit(solution)/shard_map/panel/pallas_call | solution.py:167
  40.9 4.5 %collective-permute-start.11 = (f32[512,128]{1,0:T(8,128)S(1)}, f32[512,128]{1,0:T(8,128)S(1)}, u32[]{:S(2)}, u32[]{:S(2)}) collective-permute-start(f32[512,128]{1,0:T(8,128)S(1)} %constant_dynamic-slice_fusion), channel_id=1, source_target_pairs={{0,0},{1,1},{2,2},{3,3},{36,4},{37,5},{38,6},{39,7},{72,8},{73,9},... | collective-permute-start | bytes 786440 | tf_op jit(solution)/shard_map/ppermute | solution.py:287
  45.4 1.9 %collective-permute-start.10 = (f32[512,128]{1,0:T(8,128)S(1)}, f32[512,128]{1,0:T(8,128)S(1)}, u32[]{:S(2)}, u32[]{:S(2)}) collective-permute-start(f32[512,128]{1,0:T(8,128)S(1)} %collective-permute-done.7), channel_id=1, source_target_pairs={{0,0},{1,1},{2,2},{3,3},{4,36},{5,37},{6,38},{7,39},{8,72},{9,73},... | collective-permute-start | bytes 786440 | tf_op jit(solution)/shard_map/ppermute | solution.py:287
  47.5 4.1 %collective-permute-start.13 = (f32[384,128]{1,0:T(8,128)S(1)}, f32[384,128]{1,0:T(8,128)S(1)}, u32[]{:S(2)}, u32[]{:S(2)}) collective-permute-start(f32[384,128]{1,0:T(8,128)S(1)} %add.36), channel_id=1, source_target_pairs={{0,192},{32,224},{64,128},{96,160},{128,64},{160,96},{192,0},{224,... | collective-permute-start | bytes 589832 | tf_op jit(solution)/shard_map/ppermute | solution.py:270
  51.6 6.5 %collective-permute-done.10 = f32[512,128]{1,0:T(8,128)S(1)} collective-permute-done((f32[512,128]{1,0:T(8,128)S(1)}, f32[512,128]{1,0:T(8,128)S(1)}, u32[]{:S(2)}, u32[]{:S(2)}) %collective-permute-start.10) | collective-permute-done | bytes 262176 | tf_op jit(solution)/shard_map/ppermute | solution.py:287
  58.4 7.2 %collective-permute-done.13 = f32[384,128]{1,0:T(8,128)S(1)} collective-permute-done((f32[384,128]{1,0:T(8,128)S(1)}, f32[384,128]{1,0:T(8,128)S(1)}, u32[]{:S(2)}, u32[]{:S(2)}) %collective-permute-start.13) | collective-permute-done | bytes 196640 | tf_op jit(solution)/shard_map/ppermute | solution.py:270
  65.8 0.7 collective-permute-start.16
  66.5 1.6 %collective-permute-start.17 = (f32[512,128]{1,0:T(8,128)S(1)}, f32[512,128]{1,0:T(8,128)S(1)}, u32[]{:S(2)}, u32[]{:S(2)}) collective-permute-start(f32[512,128]{1,0:T(8,128)S(1)} %collective-permute-done.10), channel_id=1, source_target_pairs={{0,1},{1,0},{2,3},{3,2},{4,5},{5,4},{6,7},{7,6},{8,9},{9,8},{10,11... | collective-permute-start | bytes 786440 | tf_op jit(solution)/shard_map/ppermute | solution.py:274
  68.1 0.9 collective-permute-start.15
  69.0 7.9 %first.1 = (f32[128,128]{1,0:T(8,128)}, f32[128,128]{1,0:T(8,128)S(1)}, f32[128,128]{1,0:T(8,128)S(1)}, f32[2048,128]{1,0:T(8,128)S(1)}, f32[128,128]{1,0:T(8,128)S(1)}) custom-call(s32[2]{0:T(128)S(1)} %pad_add_fusion.place_ref, f32[384,128]{1,0:T(8,128)S(1)} %add_add_fusion.mine_ref, f32[384,128]{1,0:T(8,128)S(1)} %collective-permute-done.14.other_ref, ...), custom_call_target="tpu_custom_call" | custom-call | flops 8589934592 | bytes 1048576 | tf_op jit(solution)/shard_map/first/pallas_call | solution.py:167
  77.0 5.8 %collective-permute-start.22 = (f32[512,128]{1,0:T(8,128)S(1)}, f32[512,128]{1,0:T(8,128)S(1)}, u32[]{:S(2)}, u32[]{:S(2)}) collective-permute-start(f32[512,128]{1,0:T(8,128)S(1)} %collective-permute-done.15), channel_id=1, source_target_pairs={{0,0},{1,1},{2,2},{3,3},{4,36},{5,37},{6,38},{7,39},{8,72},{9,73},... | collective-permute-start | bytes 786440 | tf_op jit(solution)/shard_map/ppermute | solution.py:287
  82.8 5.5 %collective-permute-start.18 = (f32[128,128]{1,0:T(8,128)S(1)}, f32[128,128]{1,0:T(8,128)S(1)}, u32[]{:S(2)}, u32[]{:S(2)}) collective-permute-start(f32[128,128]{1,0:T(8,128)S(1)} %get-tuple-element.69), channel_id=1, source_target_pairs={{0,32},{32,0},{64,96},{96,64},{128,160},{160,128},{192,224},{224,1... | collective-permute-start | bytes 196616 | tf_op jit(solution)/shard_map/ppermute | solution.py:270
  88.3 0.9 collective-permute-done.18
  89.2 3.3 %collective-permute-start.21 = (f32[128,128]{1,0:T(8,128)S(1)}, f32[128,128]{1,0:T(8,128)S(1)}, u32[]{:S(2)}, u32[]{:S(2)}) collective-permute-start(f32[128,128]{1,0:T(8,128)S(1)} %add.43.refs_0_), channel_id=1, source_target_pairs={{0,192},{32,224},{64,128},{96,160},{128,64},{160,96},{192,0},{224,... | collective-permute-start | bytes 196616 | tf_op jit(solution)/shard_map/ppermute | solution.py:270
  92.5 1.0 collective-permute-start.19
  93.4 2.9 %collective-permute-start.26 = (f32[1024,128]{1,0:T(8,128)S(1)}, f32[1024,128]{1,0:T(8,128)S(1)}, u32[]{:S(2)}, u32[]{:S(2)}) collective-permute-start(f32[1024,128]{1,0:T(8,128)S(1)} %pad_maximum_fusion.refs_4_), channel_id=1, source_target_pairs={{0,2},{1,3},{2,0},{3,1},{4,6},{5,7},{6,4},{7,5},{8,10},{9,11},{10,... | collective-permute-start | bytes 1572872 | tf_op jit(solution)/shard_map/ppermute | solution.py:274
  96.3 1.1 collective-permute-done.21.refs_3_
  97.4 1.1 collective-permute-done.20.refs_2_
  98.5 1.0 collective-permute-start.25
  99.6 2.0 %collective-permute-start.24 = (f32[512,128]{1,0:T(8,128)S(1)}, f32[512,128]{1,0:T(8,128)S(1)}, u32[]{:S(2)}, u32[]{:S(2)}) collective-permute-start(f32[512,128]{1,0:T(8,128)S(1)} %collective-permute-done.22.refs_0_), channel_id=1, source_target_pairs={{0,2},{1,3},{2,0},{3,1},{4,6},{5,7},{6,4},{7,5},{8,10},{9,11},{10,... | collective-permute-start | bytes 786440 | tf_op jit(solution)/shard_map/ppermute | solution.py:274
  101.5 1.1 collective-permute-start.23
  102.6 4.9 %second.1 = (f32[128,128]{1,0:T(8,128)S(1)}, f32[128,128]{1,0:T(8,128)}, f32[128,128]{1,0:T(8,128)S(1)}, f32[128,128]{1,0:T(8,128)S(1)}) custom-call(f32[128,128]{1,0:T(8,128)S(1)} %add.43.refs_0_, f32[128,128]{1,0:T(8,128)S(1)} %collective-permute-done.19.refs_1_, f32[128,128]{1,0:T(8,128)S(1)} %collective-permute-done.20.refs_2_, ...), custom_call_target="tpu_custom_call" | custom-call | flops 8589934592 | bytes 1048576 | tf_op jit(solution)/shard_map/second/pallas_call | solution.py:167
  107.5 6.4 %third.1 = (f32[128,128]{1,0:T(8,128)}, f32[128,128]{1,0:T(8,128)S(1)}, f32[128,128]{1,0:T(8,128)S(1)}) custom-call(f32[128,128]{1,0:T(8,128)S(1)} %get-tuple-element.77.square_ref), custom_call_target="tpu_custom_call" | custom-call | flops 8589934592 | bytes 1048576 | tf_op jit(solution)/shard_map/third/pallas_call | solution.py:167
  113.9 5.7 %collective-permute-done.25.refs_3_ = f32[512,128]{1,0:T(8,128)S(1)} collective-permute-done((f32[512,128]{1,0:T(8,128)S(1)}, f32[512,128]{1,0:T(8,128)S(1)}, u32[]{:S(2)}, u32[]{:S(2)}) %collective-permute-start.25) | collective-permute-done | bytes 262176 | tf_op jit(solution)/shard_map/ppermute | solution.py:274
  119.6 3.0 %image.1 = (f32[2048,128]{1,0:T(8,128)S(1)}, f32[2048,128]{1,0:T(8,128)S(1)}, f32[128,128]{1,0:T(8,128)S(1)}) custom-call(s32[2]{0:T(128)S(1)} %pad_add_fusion.place_ref, f32[512,128]{1,0:T(8,128)S(1)} %collective-permute-done.22.refs_0_, f32[512,128]{1,0:T(8,128)S(1)} %collective-permute-done.23.refs_1_, f32[512,128]{1,0:T(8,128)S(1)} %collective-permute-done.24.refs_2_, ...), custom_call_target="tpu_custom_call" | custom-call | flops 2147483648 | bytes 1048576 | tf_op jit(solution)/shard_map/image/pallas_call | solution.py:167
  122.8 1.2 collective-permute-done.27
  124.0 3.2 %collective-permute-start.30 = (f32[128,128]{1,0:T(8,128)S(1)}, f32[128,128]{1,0:T(8,128)S(1)}, u32[]{:S(2)}, u32[]{:S(2)}) collective-permute-start(f32[128,128]{1,0:T(8,128)S(1)} %add.44.refs_0_), channel_id=1, source_target_pairs={{0,192},{32,224},{64,128},{96,160},{128,64},{160,96},{192,0},{224,... | collective-permute-start | bytes 196616 | tf_op jit(solution)/shard_map/ppermute | solution.py:270
  127.5 1.0 collective-permute-start.28
  128.5 3.1 %left.1 = (f32[2048,128]{1,0:T(8,128)S(1)}, f32[2048,128]{1,0:T(8,128)}, f32[512,128]{1,0:T(8,128)S(1)}, f32[512,128]{1,0:T(8,128)S(1)}) custom-call(s32[2]{0:T(128)S(1)} %pad_add_fusion.place_ref, f32[2048,128]{1,0:T(8,128)S(1)} %get-tuple-element.91.base_ref, f32[512,128]{1,0:T(8,128)S(1)} %collective-permute-done.16.panel_ref, f32[512,128]{1,0:T(8,128)S(1)} %bitcast.10, ...), custom_call_target="tpu_custom_call" | custom-call | flops 2147483648 | bytes 1048576 | tf_op jit(solution)/shard_map/left/pallas_call | solution.py:167
  131.6 1.7 %collective-permute-done.29.refs_2_ = f32[128,128]{1,0:T(8,128)S(1)} collective-permute-done((f32[128,128]{1,0:T(8,128)S(1)}, f32[128,128]{1,0:T(8,128)S(1)}, u32[]{:S(2)}, u32[]{:S(2)}) %collective-permute-start.29) | collective-permute-done | bytes 65568 | tf_op jit(solution)/shard_map/ppermute | solution.py:270
  133.3 6.4 %update.1 = f32[2048,512]{1,0:T(8,128)} custom-call(f32[128,128]{1,0:T(8,128)S(1)} %add.44.refs_0_, f32[128,128]{1,0:T(8,128)S(1)} %collective-permute-done.28.refs_1_, f32[128,128]{1,0:T(8,128)S(1)} %collective-permute-done.29.refs_2_, f32[128,128]{1,0:T(8,128)S(1)} %collective-permute-done.30.refs_3_, f32[2048,512]{1,0:T(8,128)S(1)} %copy-done.1, ...), custom_call_target="tpu_custom_call" | custom-call | flops 4294967296 | bytes 1048576 | tf_op jit(solution)/shard_map/update/pallas_call | solution.py:167
  (42 shorter events, 1.9 us)
Async XLA Ops:
  3.2 9.9 %collective-permute-start.3 = (f32[512,128]{1,0:T(8,128)S(1)}, f32[512,128]{1,0:T(8,128)S(1)}, u32[]{:S(2)}, u32[]{:S(2)}) collective-permute-start(f32[512,128]{1,0:T(8,128)S(1)} %bitcast.13), channel_id=1, source_target_pairs={{0,32},{1,33},{2,34},{3,35},{4,36},{5,37},{6,38},{7,39},{8,40},{9,... | collective-permute-start | bytes 786440 | tf_op jit(solution)/shard_map/ppermute | solution.py:321
  5.0 16.8 %all-to-all-start = ((f32[8,64,128]{2,1,0:T(8,128)}), f32[8,64,128]{2,1,0:T(8,128)S(1)}, u32[]{:S(2)}, u32[]{:S(2)}) async-start(f32[8,64,128]{2,1,0:T(8,128)} %broadcast_in_dim.2), calls=%async_computation | async-start | bytes 524288 | tf_op jit(solution)/shard_map/all_to_all | solution.py:319
  13.1 12.3 %collective-permute-start.6 = (f32[512,128]{1,0:T(8,128)S(1)}, f32[512,128]{1,0:T(8,128)S(1)}, u32[]{:S(2)}, u32[]{:S(2)}) collective-permute-start(f32[512,128]{1,0:T(8,128)S(1)} %broadcast_select_fusion), channel_id=1, source_target_pairs={{0,192},{32,224},{1,193},{33,225},{2,194},{34,226},{3,195},{35,227... | collective-permute-start | bytes 786440 | tf_op jit(solution)/shard_map/ppermute | solution.py:324
  16.7 9.2 %collective-permute-start.5 = (f32[512,128]{1,0:T(8,128)S(1)}, f32[512,128]{1,0:T(8,128)S(1)}, u32[]{:S(2)}, u32[]{:S(2)}) collective-permute-start(f32[512,128]{1,0:T(8,128)S(1)} %broadcast_select_fusion), channel_id=1, source_target_pairs={{0,128},{32,160},{1,129},{33,161},{2,130},{34,162},{3,131},{35,163... | collective-permute-start | bytes 786440 | tf_op jit(solution)/shard_map/ppermute | solution.py:324
  18.1 10.6 %collective-permute-start.4 = (f32[512,128]{1,0:T(8,128)S(1)}, f32[512,128]{1,0:T(8,128)S(1)}, u32[]{:S(2)}, u32[]{:S(2)}) collective-permute-start(f32[512,128]{1,0:T(8,128)S(1)} %broadcast_select_fusion), channel_id=1, source_target_pairs={{0,64},{32,96},{1,65},{33,97},{2,66},{34,98},{3,67},{35,99},{4,68}... | collective-permute-start | bytes 786440 | tf_op jit(solution)/shard_map/ppermute | solution.py:324
  21.7 11.3 %collective-permute-start.2 = (f32[8,64,128]{2,1,0:T(8,128)S(1)}, f32[8,64,128]{2,1,0:T(8,128)S(1)}, u32[]{:S(2)}, u32[]{:S(2)}) collective-permute-start(f32[8,64,128]{2,1,0:T(8,128)S(1)} %all-to-all-done.refs_0_), channel_id=1, source_target_pairs={{0,3},{1,2},{2,1},{3,0},{4,7},{5,6},{6,5},{7,4},{8,11},{9,10},{10,... | collective-permute-start | bytes 786440 | tf_op jit(solution)/shard_map/ppermute | solution.py:274
  24.8 9.2 %collective-permute-start.1 = (f32[8,64,128]{2,1,0:T(8,128)S(1)}, f32[8,64,128]{2,1,0:T(8,128)S(1)}, u32[]{:S(2)}, u32[]{:S(2)}) collective-permute-start(f32[8,64,128]{2,1,0:T(8,128)S(1)} %all-to-all-done.refs_0_), channel_id=1, source_target_pairs={{0,2},{1,3},{2,0},{3,1},{4,6},{5,7},{6,4},{7,5},{8,10},{9,11},{10,... | collective-permute-start | bytes 786440 | tf_op jit(solution)/shard_map/ppermute | solution.py:274
  25.4 9.1 %collective-permute-start = (f32[8,64,128]{2,1,0:T(8,128)S(1)}, f32[8,64,128]{2,1,0:T(8,128)S(1)}, u32[]{:S(2)}, u32[]{:S(2)}) collective-permute-start(f32[8,64,128]{2,1,0:T(8,128)S(1)} %all-to-all-done.refs_0_), channel_id=1, source_target_pairs={{0,1},{1,0},{2,3},{3,2},{4,5},{5,4},{6,7},{7,6},{8,9},{9,8},{10,11... | collective-permute-start | bytes 786440 | tf_op jit(solution)/shard_map/ppermute | solution.py:274
  28.7 11.8 %collective-permute-start.7 = (f32[512,128]{1,0:T(8,128)S(1)}, f32[512,128]{1,0:T(8,128)S(1)}, u32[]{:S(2)}, u32[]{:S(2)}) collective-permute-start(f32[512,128]{1,0:T(8,128)S(1)} %add_select_fusion.edge_ref), channel_id=1, source_target_pairs={{0,0},{1,1},{2,2},{3,3},{4,4},{5,5},{6,6},{7,7},{8,8},{9,9},{10,10... | collective-permute-start | bytes 786440 | tf_op jit(solution)/shard_map/ppermute | solution.py:279
  34.4 2.2 %copy-start = (f32[2048,512]{1,0:T(8,128)S(1)}, f32[2048,512]{1,0:T(8,128)}, u32[]{:S(2)}) copy-start(f32[2048,512]{1,0:T(8,128)} %refs_4_.3) | copy-start | bytes 12582916
  40.5 6.9 %collective-permute-start.8 = (f32[384,128]{1,0:T(8,128)S(1)}, f32[384,128]{1,0:T(8,128)S(1)}, u32[]{:S(2)}, u32[]{:S(2)}) collective-permute-start(f32[384,128]{1,0:T(8,128)S(1)} %get-tuple-element.60), channel_id=1, source_target_pairs={{0,32},{32,0},{64,96},{96,64},{128,160},{160,128},{192,224},{224,1... | collective-permute-start | bytes 589832 | tf_op jit(solution)/shard_map/ppermute | solution.py:270
  40.9 10.7 %collective-permute-start.11 = (f32[512,128]{1,0:T(8,128)S(1)}, f32[512,128]{1,0:T(8,128)S(1)}, u32[]{:S(2)}, u32[]{:S(2)}) collective-permute-start(f32[512,128]{1,0:T(8,128)S(1)} %constant_dynamic-slice_fusion), channel_id=1, source_target_pairs={{0,0},{1,1},{2,2},{3,3},{36,4},{37,5},{38,6},{39,7},{72,8},{73,9},... | collective-permute-start | bytes 786440 | tf_op jit(solution)/shard_map/ppermute | solution.py:287
  45.4 12.7 %collective-permute-start.10 = (f32[512,128]{1,0:T(8,128)S(1)}, f32[512,128]{1,0:T(8,128)S(1)}, u32[]{:S(2)}, u32[]{:S(2)}) collective-permute-start(f32[512,128]{1,0:T(8,128)S(1)} %collective-permute-done.7), channel_id=1, source_target_pairs={{0,0},{1,1},{2,2},{3,3},{4,36},{5,37},{6,38},{7,39},{8,72},{9,73},... | collective-permute-start | bytes 786440 | tf_op jit(solution)/shard_map/ppermute | solution.py:287
  47.4 11.0 %collective-permute-start.9 = (f32[384,128]{1,0:T(8,128)S(1)}, f32[384,128]{1,0:T(8,128)S(1)}, u32[]{:S(2)}, u32[]{:S(2)}) collective-permute-start(f32[384,128]{1,0:T(8,128)S(1)} %add.36), channel_id=1, source_target_pairs={{0,64},{32,96},{64,0},{96,32},{128,192},{160,224},{192,128},{224,1... | collective-permute-start | bytes 589832 | tf_op jit(solution)/shard_map/ppermute | solution.py:270
  47.5 18.1 %collective-permute-start.13 = (f32[384,128]{1,0:T(8,128)S(1)}, f32[384,128]{1,0:T(8,128)S(1)}, u32[]{:S(2)}, u32[]{:S(2)}) collective-permute-start(f32[384,128]{1,0:T(8,128)S(1)} %add.36), channel_id=1, source_target_pairs={{0,192},{32,224},{64,128},{96,160},{128,64},{160,96},{192,0},{224,... | collective-permute-start | bytes 589832 | tf_op jit(solution)/shard_map/ppermute | solution.py:270
  51.6 14.0 %collective-permute-start.12 = (f32[384,128]{1,0:T(8,128)S(1)}, f32[384,128]{1,0:T(8,128)S(1)}, u32[]{:S(2)}, u32[]{:S(2)}) collective-permute-start(f32[384,128]{1,0:T(8,128)S(1)} %add.36), channel_id=1, source_target_pairs={{0,128},{32,160},{64,192},{96,224},{128,0},{160,32},{192,64},{224,... | collective-permute-start | bytes 589832 | tf_op jit(solution)/shard_map/ppermute | solution.py:270
  65.7 2.4 %collective-permute-start.14 = (f32[384,128]{1,0:T(8,128)S(1)}, f32[384,128]{1,0:T(8,128)S(1)}, u32[]{:S(2)}, u32[]{:S(2)}) collective-permute-start(f32[384,128]{1,0:T(8,128)S(1)} %add_add_fusion.mine_ref), channel_id=1, source_target_pairs={{0,32},{32,0},{64,96},{96,64},{128,160},{160,128},{192,224},{224,1... | collective-permute-start | bytes 589832 | tf_op jit(solution)/shard_map/ppermute | solution.py:270
  65.8 11.2 %collective-permute-start.16 = (f32[512,128]{1,0:T(8,128)S(1)}, f32[512,128]{1,0:T(8,128)S(1)}, u32[]{:S(2)}, u32[]{:S(2)}) collective-permute-start(f32[512,128]{1,0:T(8,128)S(1)} %collective-permute-done.11), channel_id=1, source_target_pairs={{0,0},{1,1},{2,2},{3,3},{4,4},{5,5},{6,6},{7,7},{8,8},{9,9},{10,10... | collective-permute-start | bytes 786440 | tf_op jit(solution)/shard_map/ppermute | solution.py:279
  66.5 10.4 %collective-permute-start.17 = (f32[512,128]{1,0:T(8,128)S(1)}, f32[512,128]{1,0:T(8,128)S(1)}, u32[]{:S(2)}, u32[]{:S(2)}) collective-permute-start(f32[512,128]{1,0:T(8,128)S(1)} %collective-permute-done.10), channel_id=1, source_target_pairs={{0,1},{1,0},{2,3},{3,2},{4,5},{5,4},{6,7},{7,6},{8,9},{9,8},{10,11... | collective-permute-start | bytes 786440 | tf_op jit(solution)/shard_map/ppermute | solution.py:274
  68.1 8.8 %collective-permute-start.15 = (f32[512,128]{1,0:T(8,128)S(1)}, f32[512,128]{1,0:T(8,128)S(1)}, u32[]{:S(2)}, u32[]{:S(2)}) collective-permute-start(f32[512,128]{1,0:T(8,128)S(1)} %bitcast.9), channel_id=1, source_target_pairs={{0,0},{1,1},{2,2},{3,3},{4,4},{5,5},{6,6},{7,7},{8,8},{9,9},{10,10... | collective-permute-start | bytes 786440 | tf_op jit(solution)/shard_map/ppermute | solution.py:279
  77.0 21.6 %collective-permute-start.22 = (f32[512,128]{1,0:T(8,128)S(1)}, f32[512,128]{1,0:T(8,128)S(1)}, u32[]{:S(2)}, u32[]{:S(2)}) collective-permute-start(f32[512,128]{1,0:T(8,128)S(1)} %collective-permute-done.15), channel_id=1, source_target_pairs={{0,0},{1,1},{2,2},{3,3},{4,36},{5,37},{6,38},{7,39},{8,72},{9,73},... | collective-permute-start | bytes 786440 | tf_op jit(solution)/shard_map/ppermute | solution.py:287
  82.8 6.4 %collective-permute-start.18 = (f32[128,128]{1,0:T(8,128)S(1)}, f32[128,128]{1,0:T(8,128)S(1)}, u32[]{:S(2)}, u32[]{:S(2)}) collective-permute-start(f32[128,128]{1,0:T(8,128)S(1)} %get-tuple-element.69), channel_id=1, source_target_pairs={{0,32},{32,0},{64,96},{96,64},{128,160},{160,128},{192,224},{224,1... | collective-permute-start | bytes 196616 | tf_op jit(solution)/shard_map/ppermute | solution.py:270
  89.2 8.3 %collective-permute-start.21 = (f32[128,128]{1,0:T(8,128)S(1)}, f32[128,128]{1,0:T(8,128)S(1)}, u32[]{:S(2)}, u32[]{:S(2)}) collective-permute-start(f32[128,128]{1,0:T(8,128)S(1)} %add.43.refs_0_), channel_id=1, source_target_pairs={{0,192},{32,224},{64,128},{96,160},{128,64},{160,96},{192,0},{224,... | collective-permute-start | bytes 196616 | tf_op jit(solution)/shard_map/ppermute | solution.py:270
  92.5 6.1 %collective-permute-start.20 = (f32[128,128]{1,0:T(8,128)S(1)}, f32[128,128]{1,0:T(8,128)S(1)}, u32[]{:S(2)}, u32[]{:S(2)}) collective-permute-start(f32[128,128]{1,0:T(8,128)S(1)} %add.43.refs_0_), channel_id=1, source_target_pairs={{0,128},{32,160},{64,192},{96,224},{128,0},{160,32},{192,64},{224,... | collective-permute-start | bytes 196616 | tf_op jit(solution)/shard_map/ppermute | solution.py:270
  92.5 6.1 %collective-permute-start.19 = (f32[128,128]{1,0:T(8,128)S(1)}, f32[128,128]{1,0:T(8,128)S(1)}, u32[]{:S(2)}, u32[]{:S(2)}) collective-permute-start(f32[128,128]{1,0:T(8,128)S(1)} %add.43.refs_0_), channel_id=1, source_target_pairs={{0,64},{32,96},{64,0},{96,32},{128,192},{160,224},{192,128},{224,1... | collective-permute-start | bytes 196616 | tf_op jit(solution)/shard_map/ppermute | solution.py:270
  93.4 26.2 %collective-permute-start.26 = (f32[1024,128]{1,0:T(8,128)S(1)}, f32[1024,128]{1,0:T(8,128)S(1)}, u32[]{:S(2)}, u32[]{:S(2)}) collective-permute-start(f32[1024,128]{1,0:T(8,128)S(1)} %pad_maximum_fusion.refs_4_), channel_id=1, source_target_pairs={{0,2},{1,3},{2,0},{3,1},{4,6},{5,7},{6,4},{7,5},{8,10},{9,11},{10,... | collective-permute-start | bytes 1572872 | tf_op jit(solution)/shard_map/ppermute | solution.py:274
  98.5 21.0 %collective-permute-start.25 = (f32[512,128]{1,0:T(8,128)S(1)}, f32[512,128]{1,0:T(8,128)S(1)}, u32[]{:S(2)}, u32[]{:S(2)}) collective-permute-start(f32[512,128]{1,0:T(8,128)S(1)} %collective-permute-done.22.refs_0_), channel_id=1, source_target_pairs={{0,3},{1,2},{2,1},{3,0},{4,7},{5,6},{6,5},{7,4},{8,11},{9,10},{10,... | collective-permute-start | bytes 786440 | tf_op jit(solution)/shard_map/ppermute | solution.py:274
  99.6 20.0 %collective-permute-start.24 = (f32[512,128]{1,0:T(8,128)S(1)}, f32[512,128]{1,0:T(8,128)S(1)}, u32[]{:S(2)}, u32[]{:S(2)}) collective-permute-start(f32[512,128]{1,0:T(8,128)S(1)} %collective-permute-done.22.refs_0_), channel_id=1, source_target_pairs={{0,2},{1,3},{2,0},{3,1},{4,6},{5,7},{6,4},{7,5},{8,10},{9,11},{10,... | collective-permute-start | bytes 786440 | tf_op jit(solution)/shard_map/ppermute | solution.py:274
  101.5 18.1 %collective-permute-start.23 = (f32[512,128]{1,0:T(8,128)S(1)}, f32[512,128]{1,0:T(8,128)S(1)}, u32[]{:S(2)}, u32[]{:S(2)}) collective-permute-start(f32[512,128]{1,0:T(8,128)S(1)} %collective-permute-done.22.refs_0_), channel_id=1, source_target_pairs={{0,1},{1,0},{2,3},{3,2},{4,5},{5,4},{6,7},{7,6},{8,9},{9,8},{10,11... | collective-permute-start | bytes 786440 | tf_op jit(solution)/shard_map/ppermute | solution.py:274
  122.7 10.7 %copy-start.1 = (f32[2048,512]{1,0:T(8,128)S(1)}, f32[2048,512]{1,0:T(8,128)}, u32[]{:S(2)}) copy-start(f32[2048,512]{1,0:T(8,128)} %refs_4_.3) | copy-start | bytes 12582916
  122.7 1.3 collective-permute-start.27
  124.0 7.6 %collective-permute-start.30 = (f32[128,128]{1,0:T(8,128)S(1)}, f32[128,128]{1,0:T(8,128)S(1)}, u32[]{:S(2)}, u32[]{:S(2)}) collective-permute-start(f32[128,128]{1,0:T(8,128)S(1)} %add.44.refs_0_), channel_id=1, source_target_pairs={{0,192},{32,224},{64,128},{96,160},{128,64},{160,96},{192,0},{224,... | collective-permute-start | bytes 196616 | tf_op jit(solution)/shard_map/ppermute | solution.py:270
  127.2 6.1 %collective-permute-start.29 = (f32[128,128]{1,0:T(8,128)S(1)}, f32[128,128]{1,0:T(8,128)S(1)}, u32[]{:S(2)}, u32[]{:S(2)}) collective-permute-start(f32[128,128]{1,0:T(8,128)S(1)} %add.44.refs_0_), channel_id=1, source_target_pairs={{0,128},{32,160},{64,192},{96,224},{128,0},{160,32},{192,64},{224,... | collective-permute-start | bytes 196616 | tf_op jit(solution)/shard_map/ppermute | solution.py:270
  127.5 5.8 %collective-permute-start.28 = (f32[128,128]{1,0:T(8,128)S(1)}, f32[128,128]{1,0:T(8,128)S(1)}, u32[]{:S(2)}, u32[]{:S(2)}) collective-permute-start(f32[128,128]{1,0:T(8,128)S(1)} %add.44.refs_0_), channel_id=1, source_target_pairs={{0,64},{32,96},{64,0},{96,32},{128,192},{160,224},{192,128},{224,1... | collective-permute-start | bytes 196616 | tf_op jit(solution)/shard_map/ppermute | solution.py:270
where the time goes:
time: 141 us; the launch traced here: 140 us
  starting transfers between devices  62.2 us (44%)
  waiting for transfers between devices  36 us (26%)
  Pallas kernels  35.5 us (25%)
  local copies, waits for them, and re-layouts  4.81 us (3%)
    pallas_call x7, Pallas kernels, block_call(): pl.pallas_call(body, out_shape=[jax.ShapeDtypeStruct(shape, jnp.float32)...  35.5 us
    ppermute x13, starting transfers between devices, swap_row(): return lax.ppermute(x, 'prow', [(r, r ^ mask) for r in range(ROWS)])  19 us
    ppermute x13, waiting for transfers between devices, swap_row(): return lax.ppermute(x, 'prow', [(r, r ^ mask) for r in range(ROWS)])  13.6 us
    ppermute x8, starting transfers between devices, swap_y(): return lax.ppermute(x, 'pcol', [(c, c ^ mask) for c in range(ZS * YS)])  12.7 us
    ppermute x3, starting transfers between devices, turn_row(): return lax.ppermute(x, ('prow', 'pcol'), moves)  12.3 us
    ppermute x8, waiting for transfers between devices, swap_y(): return lax.ppermute(x, 'pcol', [(c, c ^ mask) for c in range(ZS * YS)])  10.8 us
    all_to_all x1, starting transfers between devices, on_device(): stack = lax.all_to_all(copies, 'pcol', 0, 0, axis_index_groups=lines)  8.13 us
    ppermute x3, waiting for transfers between devices, turn_row(): return lax.ppermute(x, ('prow', 'pcol'), moves)  6.5 us
  transfers between devices with their start and end apart: 32, of which 14 were waited for; matrix products, arithmetic and copies ran while one was open for 0% of the time, Pallas kernels for 19%

commit v1 on v0

--- a/solution.py
+++ b/solution.py
@@ -188,8 +188,8 @@
 
 
 def image_kernel(place_ref, *refs):
-    products, edges = refs[:YS], refs[YS : YS + 2]
-    ortho_ref, inverse_two_ref, band_inverse_t_ref, base_ref, image_ref, weight_ref = refs[YS + 2 :]
+    products, edges = refs[:YS], refs[YS : 2 * YS]
+    ortho_ref, inverse_two_ref, band_inverse_t_ref, base_ref, image_ref, weight_ref = refs[2 * YS :]
     cols, width = products[0].shape
     y = place_ref[1] % YS
     inverse_two = split(inverse_two_ref[...])
@@ -200,7 +200,7 @@
         span = pl.ds(at, cols)
         start = place_ref[0] * (YS * cols) + at
         base = dot_split(split(ortho_ref[span, :]), inverse_two, NT) + unit_rows(start, cols, width)
-        image = dot(products[far][...], band_inverse_t, NT) + edges[far // 2][(far % 2) * cols : (far % 2 + 1) * cols, :]
+        image = dot(products[far][...], band_inverse_t, NT) + edges[far][...]
         base_ref[span, :] = base
         image_ref[span, :] = image
         weight = weight + dot_split(split(base), split(image), TN)
@@ -344,8 +344,7 @@
     panel_cols = lax.dynamic_slice_in_dim(panel_rows, y * cols, cols, 0)
     panel_cols = turn_row(panel_cols, back=True)
     messages[1], edge_turned, panel_cols = hold(messages[1], edge_turned, panel_cols)
-    edge_pair = jnp.concatenate([edge_turned, swap_y(edge_turned, 1)], 0)
-    panel_cols = turn_z(panel_cols)
+    edges = along_y(edge_turned)
 
     mine = (messages[0] + messages[1]) + (messages[2] + messages[3])
     mine, other = hold(mine, swap_row(mine, 1))
@@ -364,15 +363,15 @@
         in_specs=[scalars()] + whole(3),
         out_specs=whole(5),
     )
-    gram, product_turned, panel_cols, edge_pair = hold(gram, product_turned, panel_cols, edge_pair)
-
-    gram = gram + swap_row(gram, 1)
+    gram, product_turned, *edges = hold(gram, product_turned, *edges)
+
+    gram, product_turned = hold(gram + swap_row(gram, 1), product_turned)
     product_turned = turn_row(product_turned)
+    panel_cols = turn_z(panel_cols)
     grams = three_rows(gram)
-    *grams, product_turned = hold(*grams, product_turned)
+    *grams, product_turned, panel_cols = hold(*grams, product_turned, panel_cols)
 
     turned = along_y(product_turned)
-    edges = [edge_pair, swap_y(edge_pair, 2)]
     inverse_two, band_block, band_inverse_t, top = block_call(
         second_kernel, [square] * 4, "second", 1 << 33, grams + [upper_copy, inverse_one, leading],
         in_specs=whole(7), out_specs=whole(4),
@@ -387,7 +386,7 @@
         "image",
         1 << 31,
         [place] + turned + edges + [ortho_rows, inverse_two, band_inverse_t],
-        in_specs=[scalars()] + whole(YS + 5),
+        in_specs=[scalars()] + whole(2 * YS + 3),
         out_specs=whole(3),
     )
 

time: 141 us -> 136 us (0.965)
  starting transfers between devices: 62.2 us -> 56.9 us
    ppermute x3, starting transfers between devices: 12.3 us -> 8.37 us  [turn_row(): return lax.ppermute(x, ('prow', 'pcol'), moves)]
    ppermute x13, waiting for transfers between devices: 13.6 us -> 16.8 us  [swap_row(): return lax.ppermute(x, 'prow', [(r, r ^ mask) for r in range(ROWS)])]
    ppermute x8 -> x9, waiting for transfers between devices: 10.8 us -> 8.23 us  [swap_y(): return lax.ppermute(x, 'pcol', [(c, c ^ mask) for c in range(ZS * YS)])]
    ppermute x8 -> x9, starting transfers between devices: 12.7 us -> 12.5 us  [swap_y(): return lax.ppermute(x, 'pcol', [(c, c ^ mask) for c in range(ZS * YS)])]
  transfers between devices with their start and end apart: 32 -> 33, of which waited for: 14 -> 14; matrix products, arithmetic and copies ran while one was open for 0% -> 0% of each run, Pallas kernels for 19% -> 19%
where the time goes in v1:
time: 136 us; the launch traced here: 135 us
  starting transfers between devices  56.9 us (42%)
  waiting for transfers between devices  36.6 us (27%)
  Pallas kernels  35.5 us (26%)
  local copies, waits for them, and re-layouts  4.81 us (4%)
    pallas_call x7, Pallas kernels, block_call(): pl.pallas_call(body, out_shape=[jax.ShapeDtypeStruct(shape, jnp.float32)...  35.5 us
    ppermute x13, starting transfers between devices, swap_row(): return lax.ppermute(x, 'prow', [(r, r ^ mask) for r in range(ROWS)])  17.8 us
    ppermute x13, waiting for transfers between devices, swap_row(): return lax.ppermute(x, 'prow', [(r, r ^ mask) for r in range(ROWS)])  16.8 us
    ppermute x9, starting transfers between devices, swap_y(): return lax.ppermute(x, 'pcol', [(c, c ^ mask) for c in range(ZS * YS)])  12.5 us
    ppermute x3, starting transfers between devices, turn_row(): return lax.ppermute(x, ('prow', 'pcol'), moves)  8.37 us
    ppermute x9, waiting for transfers between devices, swap_y(): return lax.ppermute(x, 'pcol', [(c, c ^ mask) for c in range(ZS * YS)])  8.23 us
    all_to_all x1, starting transfers between devices, on_device(): stack = lax.all_to_all(copies, 'pcol', 0, 0, axis_index_groups=lines)  8.13 us
    ppermute x3, waiting for transfers between devices, turn_row(): return lax.ppermute(x, ('prow', 'pcol'), moves)  6.51 us
  transfers between devices with their start and end apart: 33, of which 14 were waited for; matrix products, arithmetic and copies ran while one was open for 0% of the time, Pallas kernels for 19%

profile of v1, /device:TPU:64, one launch (start us, length us, event | category | flops | bytes accessed | tf_op | source)
XLA Modules:
  0.0 135.1 jit_solution(17581207426368555831)
XLA Ops:
  0.6 1.0 slice.9
  1.7 1.5 %broadcast_in_dim.2 = f32[8,64,128]{2,1,0:T(8,128)} broadcast(f32[64,128]{1,0:T(8,128)} %param.3), dimensions={1,2} | broadcast | bytes 294912 | tf_op jit(solution)/shard_map/broadcast_in_dim | solution.py:317
  3.2 1.7 %collective-permute-start.3 = (f32[512,128]{1,0:T(8,128)S(1)}, f32[512,128]{1,0:T(8,128)S(1)}, u32[]{:S(2)}, u32[]{:S(2)}) collective-permute-start(f32[512,128]{1,0:T(8,128)S(1)} %bitcast.13), channel_id=1, source_target_pairs={{0,32},{1,33},{2,34},{3,35},{4,36},{5,37},{6,38},{7,39},{8,40},{9,... | collective-permute-start | bytes 786440 | tf_op jit(solution)/shard_map/ppermute | solution.py:321
  5.0 8.1 %all-to-all-start = ((f32[8,64,128]{2,1,0:T(8,128)}), f32[8,64,128]{2,1,0:T(8,128)S(1)}, u32[]{:S(2)}, u32[]{:S(2)}) async-start(f32[8,64,128]{2,1,0:T(8,128)} %broadcast_in_dim.2), calls=%async_computation | async-start | bytes 524288 | tf_op jit(solution)/shard_map/all_to_all | solution.py:319
  13.1 3.6 %collective-permute-start.6 = (f32[512,128]{1,0:T(8,128)S(1)}, f32[512,128]{1,0:T(8,128)S(1)}, u32[]{:S(2)}, u32[]{:S(2)}) collective-permute-start(f32[512,128]{1,0:T(8,128)S(1)} %broadcast_select_fusion), channel_id=1, source_target_pairs={{0,192},{32,224},{1,193},{33,225},{2,194},{34,226},{3,195},{35,227... | collective-permute-start | bytes 786440 | tf_op jit(solution)/shard_map/ppermute | solution.py:324
  16.7 1.3 collective-permute-start.5
  18.1 1.3 collective-permute-start.4
  19.4 2.4 %all-to-all-done.refs_0_ = f32[8,64,128]{2,1,0:T(8,128)S(1)} async-done(((f32[8,64,128]{2,1,0:T(8,128)}), f32[8,64,128]{2,1,0:T(8,128)S(1)}, u32[]{:S(2)}, u32[]{:S(2)}) %all-to-all-start) | async-done | bytes 262176 | tf_op jit(solution)/shard_map/all_to_all | solution.py:319
  21.7 3.0 %collective-permute-start.2 = (f32[8,64,128]{2,1,0:T(8,128)S(1)}, f32[8,64,128]{2,1,0:T(8,128)S(1)}, u32[]{:S(2)}, u32[]{:S(2)}) collective-permute-start(f32[8,64,128]{2,1,0:T(8,128)S(1)} %all-to-all-done.refs_0_), channel_id=1, source_target_pairs={{0,3},{1,2},{2,1},{3,0},{4,7},{5,6},{6,5},{7,4},{8,11},{9,10},{10,... | collective-permute-start | bytes 786440 | tf_op jit(solution)/shard_map/ppermute | solution.py:274
  24.8 0.6 collective-permute-start.1
  25.4 0.5 collective-permute-start
  25.9 2.7 %collective-permute-done.4 = f32[512,128]{1,0:T(8,128)S(1)} collective-permute-done((f32[512,128]{1,0:T(8,128)S(1)}, f32[512,128]{1,0:T(8,128)S(1)}, u32[]{:S(2)}, u32[]{:S(2)}) %collective-permute-start.4) | collective-permute-done | bytes 262176 | tf_op jit(solution)/shard_map/ppermute | solution.py:324
  28.7 0.7 collective-permute-start.7
  29.4 3.7 %collective-permute-done.2.refs_3_ = f32[8,64,128]{2,1,0:T(8,128)S(1)} collective-permute-done((f32[8,64,128]{2,1,0:T(8,128)S(1)}, f32[8,64,128]{2,1,0:T(8,128)S(1)}, u32[]{:S(2)}, u32[]{:S(2)}) %collective-permute-start.2) | collective-permute-done | bytes 262176 | tf_op jit(solution)/shard_map/ppermute | solution.py:274
  33.0 0.9 collective-permute-done.1.refs_2_
  34.0 0.5 collective-permute-done.refs_1_
  34.4 2.2 %copy-done = f32[2048,512]{1,0:T(8,128)S(1)} copy-done((f32[2048,512]{1,0:T(8,128)S(1)}, f32[2048,512]{1,0:T(8,128)}, u32[]{:S(2)}) %copy-start) | copy-done | bytes 4194328
  36.6 3.8 %panel.1 = (f32[2048,128]{1,0:T(8,128)S(1)}, f32[384,128]{1,0:T(8,128)S(1)}, f32[384,128]{1,0:T(8,128)S(1)}) custom-call(s32[2]{0:T(128)S(1)} %pad_add_fusion.place_ref, f32[8,64,128]{2,1,0:T(8,128)S(1)} %all-to-all-done.refs_0_, f32[8,64,128]{2,1,0:T(8,128)S(1)} %collective-permute-done.refs_1_, f32[8,64,128]{2,1,0:T(8,128)S(1)} %collective-permute-done.1.refs_2_, ...), custom_call_target="tpu_custom_call" | custom-call | flops 4294967296 | bytes 1048576 | tf_op jit(solution)/shard_map/panel/pallas_call | solution.py:167
  40.9 4.5 %collective-permute-start.11 = (f32[512,128]{1,0:T(8,128)S(1)}, f32[512,128]{1,0:T(8,128)S(1)}, u32[]{:S(2)}, u32[]{:S(2)}) collective-permute-start(f32[512,128]{1,0:T(8,128)S(1)} %constant_dynamic-slice_fusion), channel_id=1, source_target_pairs={{0,0},{1,1},{2,2},{3,3},{36,4},{37,5},{38,6},{39,7},{72,8},{73,9},... | collective-permute-start | bytes 786440 | tf_op jit(solution)/shard_map/ppermute | solution.py:287
  45.4 1.9 %collective-permute-start.10 = (f32[512,128]{1,0:T(8,128)S(1)}, f32[512,128]{1,0:T(8,128)S(1)}, u32[]{:S(2)}, u32[]{:S(2)}) collective-permute-start(f32[512,128]{1,0:T(8,128)S(1)} %collective-permute-done.7), channel_id=1, source_target_pairs={{0,0},{1,1},{2,2},{3,3},{4,36},{5,37},{6,38},{7,39},{8,72},{9,73},... | collective-permute-start | bytes 786440 | tf_op jit(solution)/shard_map/ppermute | solution.py:287
  47.5 4.1 %collective-permute-start.13 = (f32[384,128]{1,0:T(8,128)S(1)}, f32[384,128]{1,0:T(8,128)S(1)}, u32[]{:S(2)}, u32[]{:S(2)}) collective-permute-start(f32[384,128]{1,0:T(8,128)S(1)} %add.36), channel_id=1, source_target_pairs={{0,192},{32,224},{64,128},{96,160},{128,64},{160,96},{192,0},{224,... | collective-permute-start | bytes 589832 | tf_op jit(solution)/shard_map/ppermute | solution.py:270
  51.6 6.5 %collective-permute-done.10.refs_4_ = f32[512,128]{1,0:T(8,128)S(1)} collective-permute-done((f32[512,128]{1,0:T(8,128)S(1)}, f32[512,128]{1,0:T(8,128)S(1)}, u32[]{:S(2)}, u32[]{:S(2)}) %collective-permute-start.10) | collective-permute-done | bytes 262176 | tf_op jit(solution)/shard_map/ppermute | solution.py:287
  58.4 7.2 %collective-permute-done.13 = f32[384,128]{1,0:T(8,128)S(1)} collective-permute-done((f32[384,128]{1,0:T(8,128)S(1)}, f32[384,128]{1,0:T(8,128)S(1)}, u32[]{:S(2)}, u32[]{:S(2)}) %collective-permute-start.13) | collective-permute-done | bytes 196640 | tf_op jit(solution)/shard_map/ppermute | solution.py:270
  65.8 3.0 %collective-permute-start.18 = (f32[512,128]{1,0:T(8,128)S(1)}, f32[512,128]{1,0:T(8,128)S(1)}, u32[]{:S(2)}, u32[]{:S(2)}) collective-permute-start(f32[512,128]{1,0:T(8,128)S(1)} %collective-permute-done.10.refs_4_), channel_id=1, source_target_pairs={{0,3},{1,2},{2,1},{3,0},{4,7},{5,6},{6,5},{7,4},{8,11},{9,10},{10,... | collective-permute-start | bytes 786440 | tf_op jit(solution)/shard_map/ppermute | solution.py:274
  68.8 0.6 collective-permute-start.17
  69.4 0.5 collective-permute-start.16
  70.0 0.9 collective-permute-start.15
  70.9 7.9 %first.1 = (f32[128,128]{1,0:T(8,128)}, f32[128,128]{1,0:T(8,128)S(1)}, f32[128,128]{1,0:T(8,128)S(1)}, f32[2048,128]{1,0:T(8,128)S(1)}, f32[128,128]{1,0:T(8,128)S(1)}) custom-call(s32[2]{0:T(128)S(1)} %pad_add_fusion.place_ref, f32[384,128]{1,0:T(8,128)S(1)} %add_add_fusion.mine_ref, f32[384,128]{1,0:T(8,128)S(1)} %collective-permute-done.14.other_ref, ...), custom_call_target="tpu_custom_call" | custom-call | flops 8589934592 | bytes 1048576 | tf_op jit(solution)/shard_map/first/pallas_call | solution.py:167
  78.8 2.5 %collective-permute-done.18.refs_7_ = f32[512,128]{1,0:T(8,128)S(1)} collective-permute-done((f32[512,128]{1,0:T(8,128)S(1)}, f32[512,128]{1,0:T(8,128)S(1)}, u32[]{:S(2)}, u32[]{:S(2)}) %collective-permute-start.18) | collective-permute-done | bytes 262176 | tf_op jit(solution)/shard_map/ppermute | solution.py:274
  81.3 0.6 collective-permute-done.16.refs_5_
  82.0 0.9 collective-permute-start.19
  82.9 0.7 collective-permute-start.24
  83.8 1.9 %collective-permute-start.23 = (f32[512,128]{1,0:T(8,128)S(1)}, f32[512,128]{1,0:T(8,128)S(1)}, u32[]{:S(2)}, u32[]{:S(2)}) collective-permute-start(f32[512,128]{1,0:T(8,128)S(1)} %collective-permute-done.15), channel_id=1, source_target_pairs={{0,0},{1,1},{2,2},{3,3},{4,36},{5,37},{6,38},{7,39},{8,72},{9,73},... | collective-permute-start | bytes 786440 | tf_op jit(solution)/shard_map/ppermute | solution.py:287
  85.7 6.7 %collective-permute-start.22 = (f32[128,128]{1,0:T(8,128)S(1)}, f32[128,128]{1,0:T(8,128)S(1)}, u32[]{:S(2)}, u32[]{:S(2)}) collective-permute-start(f32[128,128]{1,0:T(8,128)S(1)} %add.43.refs_0_), channel_id=1, source_target_pairs={{0,192},{32,224},{64,128},{96,160},{128,64},{160,96},{192,0},{224,... | collective-permute-start | bytes 196616 | tf_op jit(solution)/shard_map/ppermute | solution.py:270
  92.4 1.0 collective-permute-start.20
  93.3 5.8 %collective-permute-done.22.refs_3_ = f32[128,128]{1,0:T(8,128)S(1)} collective-permute-done((f32[128,128]{1,0:T(8,128)S(1)}, f32[128,128]{1,0:T(8,128)S(1)}, u32[]{:S(2)}, u32[]{:S(2)}) %collective-permute-start.22) | collective-permute-done | bytes 65568 | tf_op jit(solution)/shard_map/ppermute | solution.py:270
  99.2 3.0 %collective-permute-start.27 = (f32[512,128]{1,0:T(8,128)S(1)}, f32[512,128]{1,0:T(8,128)S(1)}, u32[]{:S(2)}, u32[]{:S(2)}) collective-permute-start(f32[512,128]{1,0:T(8,128)S(1)} %collective-permute-done.23.refs_0_), channel_id=1, source_target_pairs={{0,3},{1,2},{2,1},{3,0},{4,7},{5,6},{6,5},{7,4},{8,11},{9,10},{10,... | collective-permute-start | bytes 786440 | tf_op jit(solution)/shard_map/ppermute | solution.py:274
  102.2 0.6 collective-permute-start.26
  102.8 0.5 collective-permute-start.25
  103.4 4.9 %second.1 = (f32[128,128]{1,0:T(8,128)S(1)}, f32[128,128]{1,0:T(8,128)}, f32[128,128]{1,0:T(8,128)S(1)}, f32[128,128]{1,0:T(8,128)S(1)}) custom-call(f32[128,128]{1,0:T(8,128)S(1)} %add.43.refs_0_, f32[128,128]{1,0:T(8,128)S(1)} %collective-permute-done.20.refs_1_, f32[128,128]{1,0:T(8,128)S(1)} %collective-permute-done.21.refs_2_, ...), custom_call_target="tpu_custom_call" | custom-call | flops 8589934592 | bytes 1048576 | tf_op jit(solution)/shard_map/second/pallas_call | solution.py:167
  108.2 6.4 %third.1 = (f32[128,128]{1,0:T(8,128)}, f32[128,128]{1,0:T(8,128)S(1)}, f32[128,128]{1,0:T(8,128)S(1)}) custom-call(f32[128,128]{1,0:T(8,128)S(1)} %get-tuple-element.84.square_ref), custom_call_target="tpu_custom_call" | custom-call | flops 8589934592 | bytes 1048576 | tf_op jit(solution)/shard_map/third/pallas_call | solution.py:167
  114.6 3.0 %image.1 = (f32[2048,128]{1,0:T(8,128)S(1)}, f32[2048,128]{1,0:T(8,128)S(1)}, f32[128,128]{1,0:T(8,128)S(1)}) custom-call(s32[2]{0:T(128)S(1)} %pad_add_fusion.place_ref, f32[512,128]{1,0:T(8,128)S(1)} %collective-permute-done.23.refs_0_, f32[512,128]{1,0:T(8,128)S(1)} %collective-permute-done.25.refs_1_, f32[512,128]{1,0:T(8,128)S(1)} %collective-permute-done.26.refs_2_, ...), custom_call_target="tpu_custom_call" | custom-call | flops 2147483648 | bytes 1048576 | tf_op jit(solution)/shard_map/image/pallas_call | solution.py:167
  117.8 1.2 collective-permute-done.28
  119.0 3.5 %collective-permute-start.31 = (f32[128,128]{1,0:T(8,128)S(1)}, f32[128,128]{1,0:T(8,128)S(1)}, u32[]{:S(2)}, u32[]{:S(2)}) collective-permute-start(f32[128,128]{1,0:T(8,128)S(1)} %add.44.refs_0_), channel_id=1, source_target_pairs={{0,192},{32,224},{64,128},{96,160},{128,64},{160,96},{192,0},{224,... | collective-permute-start | bytes 196616 | tf_op jit(solution)/shard_map/ppermute | solution.py:270
  122.6 1.0 collective-permute-start.29
  123.5 3.1 %left.1 = (f32[2048,128]{1,0:T(8,128)S(1)}, f32[2048,128]{1,0:T(8,128)}, f32[512,128]{1,0:T(8,128)S(1)}, f32[512,128]{1,0:T(8,128)S(1)}) custom-call(s32[2]{0:T(128)S(1)} %pad_add_fusion.place_ref, f32[2048,128]{1,0:T(8,128)S(1)} %get-tuple-element.101.base_ref, f32[512,128]{1,0:T(8,128)S(1)} %collective-permute-done.24.panel_ref, f32[512,128]{1,0:T(8,128)S(1)} %bitcast.10, ...), custom_call_target="tpu_custom_call" | custom-call | flops 2147483648 | bytes 1048576 | tf_op jit(solution)/shard_map/left/pallas_call | solution.py:167
  126.6 2.0 %collective-permute-done.30.refs_2_ = f32[128,128]{1,0:T(8,128)S(1)} collective-permute-done((f32[128,128]{1,0:T(8,128)S(1)}, f32[128,128]{1,0:T(8,128)S(1)}, u32[]{:S(2)}, u32[]{:S(2)}) %collective-permute-start.30) | collective-permute-done | bytes 65568 | tf_op jit(solution)/shard_map/ppermute | solution.py:270
  128.7 6.4 %update.1 = f32[2048,512]{1,0:T(8,128)} custom-call(f32[128,128]{1,0:T(8,128)S(1)} %add.44.refs_0_, f32[128,128]{1,0:T(8,128)S(1)} %collective-permute-done.29.refs_1_, f32[128,128]{1,0:T(8,128)S(1)} %collective-permute-done.30.refs_2_, f32[128,128]{1,0:T(8,128)S(1)} %collective-permute-done.31.refs_3_, f32[2048,512]{1,0:T(8,128)S(1)} %copy-done.1, ...), custom_call_target="tpu_custom_call" | custom-call | flops 4294967296 | bytes 1048576 | tf_op jit(solution)/shard_map/update/pallas_call | solution.py:167
  (43 shorter events, 1.8 us)
Async XLA Ops:
  3.2 9.9 %collective-permute-start.3 = (f32[512,128]{1,0:T(8,128)S(1)}, f32[512,128]{1,0:T(8,128)S(1)}, u32[]{:S(2)}, u32[]{:S(2)}) collective-permute-start(f32[512,128]{1,0:T(8,128)S(1)} %bitcast.13), channel_id=1, source_target_pairs={{0,32},{1,33},{2,34},{3,35},{4,36},{5,37},{6,38},{7,39},{8,40},{9,... | collective-permute-start | bytes 786440 | tf_op jit(solution)/shard_map/ppermute | solution.py:321
  5.0 16.8 %all-to-all-start = ((f32[8,64,128]{2,1,0:T(8,128)}), f32[8,64,128]{2,1,0:T(8,128)S(1)}, u32[]{:S(2)}, u32[]{:S(2)}) async-start(f32[8,64,128]{2,1,0:T(8,128)} %broadcast_in_dim.2), calls=%async_computation | async-start | bytes 524288 | tf_op jit(solution)/shard_map/all_to_all | solution.py:319
  13.1 12.3 %collective-permute-start.6 = (f32[512,128]{1,0:T(8,128)S(1)}, f32[512,128]{1,0:T(8,128)S(1)}, u32[]{:S(2)}, u32[]{:S(2)}) collective-permute-start(f32[512,128]{1,0:T(8,128)S(1)} %broadcast_select_fusion), channel_id=1, source_target_pairs={{0,192},{32,224},{1,193},{33,225},{2,194},{34,226},{3,195},{35,227... | collective-permute-start | bytes 786440 | tf_op jit(solution)/shard_map/ppermute | solution.py:324
  16.7 9.2 %collective-permute-start.5 = (f32[512,128]{1,0:T(8,128)S(1)}, f32[512,128]{1,0:T(8,128)S(1)}, u32[]{:S(2)}, u32[]{:S(2)}) collective-permute-start(f32[512,128]{1,0:T(8,128)S(1)} %broadcast_select_fusion), channel_id=1, source_target_pairs={{0,128},{32,160},{1,129},{33,161},{2,130},{34,162},{3,131},{35,163... | collective-permute-start | bytes 786440 | tf_op jit(solution)/shard_map/ppermute | solution.py:324
  18.1 10.6 %collective-permute-start.4 = (f32[512,128]{1,0:T(8,128)S(1)}, f32[512,128]{1,0:T(8,128)S(1)}, u32[]{:S(2)}, u32[]{:S(2)}) collective-permute-start(f32[512,128]{1,0:T(8,128)S(1)} %broadcast_select_fusion), channel_id=1, source_target_pairs={{0,64},{32,96},{1,65},{33,97},{2,66},{34,98},{3,67},{35,99},{4,68}... | collective-permute-start | bytes 786440 | tf_op jit(solution)/shard_map/ppermute | solution.py:324
  21.7 11.3 %collective-permute-start.2 = (f32[8,64,128]{2,1,0:T(8,128)S(1)}, f32[8,64,128]{2,1,0:T(8,128)S(1)}, u32[]{:S(2)}, u32[]{:S(2)}) collective-permute-start(f32[8,64,128]{2,1,0:T(8,128)S(1)} %all-to-all-done.refs_0_), channel_id=1, source_target_pairs={{0,3},{1,2},{2,1},{3,0},{4,7},{5,6},{6,5},{7,4},{8,11},{9,10},{10,... | collective-permute-start | bytes 786440 | tf_op jit(solution)/shard_map/ppermute | solution.py:274
  24.8 9.2 %collective-permute-start.1 = (f32[8,64,128]{2,1,0:T(8,128)S(1)}, f32[8,64,128]{2,1,0:T(8,128)S(1)}, u32[]{:S(2)}, u32[]{:S(2)}) collective-permute-start(f32[8,64,128]{2,1,0:T(8,128)S(1)} %all-to-all-done.refs_0_), channel_id=1, source_target_pairs={{0,2},{1,3},{2,0},{3,1},{4,6},{5,7},{6,4},{7,5},{8,10},{9,11},{10,... | collective-permute-start | bytes 786440 | tf_op jit(solution)/shard_map/ppermute | solution.py:274
  25.4 9.1 %collective-permute-start = (f32[8,64,128]{2,1,0:T(8,128)S(1)}, f32[8,64,128]{2,1,0:T(8,128)S(1)}, u32[]{:S(2)}, u32[]{:S(2)}) collective-permute-start(f32[8,64,128]{2,1,0:T(8,128)S(1)} %all-to-all-done.refs_0_), channel_id=1, source_target_pairs={{0,1},{1,0},{2,3},{3,2},{4,5},{5,4},{6,7},{7,6},{8,9},{9,8},{10,11... | collective-permute-start | bytes 786440 | tf_op jit(solution)/shard_map/ppermute | solution.py:274
  28.7 11.8 %collective-permute-start.7 = (f32[512,128]{1,0:T(8,128)S(1)}, f32[512,128]{1,0:T(8,128)S(1)}, u32[]{:S(2)}, u32[]{:S(2)}) collective-permute-start(f32[512,128]{1,0:T(8,128)S(1)} %add_select_fusion.edge_ref), channel_id=1, source_target_pairs={{0,0},{1,1},{2,2},{3,3},{4,4},{5,5},{6,6},{7,7},{8,8},{9,9},{10,10... | collective-permute-start | bytes 786440 | tf_op jit(solution)/shard_map/ppermute | solution.py:279
  34.4 2.2 %copy-start = (f32[2048,512]{1,0:T(8,128)S(1)}, f32[2048,512]{1,0:T(8,128)}, u32[]{:S(2)}) copy-start(f32[2048,512]{1,0:T(8,128)} %refs_4_.3) | copy-start | bytes 12582916
  40.5 6.9 %collective-permute-start.8 = (f32[384,128]{1,0:T(8,128)S(1)}, f32[384,128]{1,0:T(8,128)S(1)}, u32[]{:S(2)}, u32[]{:S(2)}) collective-permute-start(f32[384,128]{1,0:T(8,128)S(1)} %get-tuple-element.65), channel_id=1, source_target_pairs={{0,32},{32,0},{64,96},{96,64},{128,160},{160,128},{192,224},{224,1... | collective-permute-start | bytes 589832 | tf_op jit(solution)/shard_map/ppermute | solution.py:270
  40.9 10.7 %collective-permute-start.11 = (f32[512,128]{1,0:T(8,128)S(1)}, f32[512,128]{1,0:T(8,128)S(1)}, u32[]{:S(2)}, u32[]{:S(2)}) collective-permute-start(f32[512,128]{1,0:T(8,128)S(1)} %constant_dynamic-slice_fusion), channel_id=1, source_target_pairs={{0,0},{1,1},{2,2},{3,3},{36,4},{37,5},{38,6},{39,7},{72,8},{73,9},... | collective-permute-start | bytes 786440 | tf_op jit(solution)/shard_map/ppermute | solution.py:287
  45.4 12.7 %collective-permute-start.10 = (f32[512,128]{1,0:T(8,128)S(1)}, f32[512,128]{1,0:T(8,128)S(1)}, u32[]{:S(2)}, u32[]{:S(2)}) collective-permute-start(f32[512,128]{1,0:T(8,128)S(1)} %collective-permute-done.7), channel_id=1, source_target_pairs={{0,0},{1,1},{2,2},{3,3},{4,36},{5,37},{6,38},{7,39},{8,72},{9,73},... | collective-permute-start | bytes 786440 | tf_op jit(solution)/shard_map/ppermute | solution.py:287
  47.4 11.0 %collective-permute-start.9 = (f32[384,128]{1,0:T(8,128)S(1)}, f32[384,128]{1,0:T(8,128)S(1)}, u32[]{:S(2)}, u32[]{:S(2)}) collective-permute-start(f32[384,128]{1,0:T(8,128)S(1)} %add.36), channel_id=1, source_target_pairs={{0,64},{32,96},{64,0},{96,32},{128,192},{160,224},{192,128},{224,1... | collective-permute-start | bytes 589832 | tf_op jit(solution)/shard_map/ppermute | solution.py:270
  47.5 18.1 %collective-permute-start.13 = (f32[384,128]{1,0:T(8,128)S(1)}, f32[384,128]{1,0:T(8,128)S(1)}, u32[]{:S(2)}, u32[]{:S(2)}) collective-permute-start(f32[384,128]{1,0:T(8,128)S(1)} %add.36), channel_id=1, source_target_pairs={{0,192},{32,224},{64,128},{96,160},{128,64},{160,96},{192,0},{224,... | collective-permute-start | bytes 589832 | tf_op jit(solution)/shard_map/ppermute | solution.py:270
  51.6 14.0 %collective-permute-start.12 = (f32[384,128]{1,0:T(8,128)S(1)}, f32[384,128]{1,0:T(8,128)S(1)}, u32[]{:S(2)}, u32[]{:S(2)}) collective-permute-start(f32[384,128]{1,0:T(8,128)S(1)} %add.36), channel_id=1, source_target_pairs={{0,128},{32,160},{64,192},{96,224},{128,0},{160,32},{192,64},{224,... | collective-permute-start | bytes 589832 | tf_op jit(solution)/shard_map/ppermute | solution.py:270
  65.7 4.3 %collective-permute-start.14 = (f32[384,128]{1,0:T(8,128)S(1)}, f32[384,128]{1,0:T(8,128)S(1)}, u32[]{:S(2)}, u32[]{:S(2)}) collective-permute-start(f32[384,128]{1,0:T(8,128)S(1)} %add_add_fusion.mine_ref), channel_id=1, source_target_pairs={{0,32},{32,0},{64,96},{96,64},{128,160},{160,128},{192,224},{224,1... | collective-permute-start | bytes 589832 | tf_op jit(solution)/shard_map/ppermute | solution.py:270
  65.8 15.6 %collective-permute-start.18 = (f32[512,128]{1,0:T(8,128)S(1)}, f32[512,128]{1,0:T(8,128)S(1)}, u32[]{:S(2)}, u32[]{:S(2)}) collective-permute-start(f32[512,128]{1,0:T(8,128)S(1)} %collective-permute-done.10.refs_4_), channel_id=1, source_target_pairs={{0,3},{1,2},{2,1},{3,0},{4,7},{5,6},{6,5},{7,4},{8,11},{9,10},{10,... | collective-permute-start | bytes 786440 | tf_op jit(solution)/shard_map/ppermute | solution.py:274
  68.8 12.5 %collective-permute-start.17 = (f32[512,128]{1,0:T(8,128)S(1)}, f32[512,128]{1,0:T(8,128)S(1)}, u32[]{:S(2)}, u32[]{:S(2)}) collective-permute-start(f32[512,128]{1,0:T(8,128)S(1)} %collective-permute-done.10.refs_4_), channel_id=1, source_target_pairs={{0,2},{1,3},{2,0},{3,1},{4,6},{5,7},{6,4},{7,5},{8,10},{9,11},{10,... | collective-permute-start | bytes 786440 | tf_op jit(solution)/shard_map/ppermute | solution.py:274
  69.4 12.5 %collective-permute-start.16 = (f32[512,128]{1,0:T(8,128)S(1)}, f32[512,128]{1,0:T(8,128)S(1)}, u32[]{:S(2)}, u32[]{:S(2)}) collective-permute-start(f32[512,128]{1,0:T(8,128)S(1)} %collective-permute-done.10.refs_4_), channel_id=1, source_target_pairs={{0,1},{1,0},{2,3},{3,2},{4,5},{5,4},{6,7},{7,6},{8,9},{9,8},{10,11... | collective-permute-start | bytes 786440 | tf_op jit(solution)/shard_map/ppermute | solution.py:274
  70.0 11.9 %collective-permute-start.15 = (f32[512,128]{1,0:T(8,128)S(1)}, f32[512,128]{1,0:T(8,128)S(1)}, u32[]{:S(2)}, u32[]{:S(2)}) collective-permute-start(f32[512,128]{1,0:T(8,128)S(1)} %bitcast.9), channel_id=1, source_target_pairs={{0,0},{1,1},{2,2},{3,3},{4,4},{5,5},{6,6},{7,7},{8,8},{9,9},{10,10... | collective-permute-start | bytes 786440 | tf_op jit(solution)/shard_map/ppermute | solution.py:279
  82.0 1.8 %collective-permute-start.19 = (f32[128,128]{1,0:T(8,128)S(1)}, f32[128,128]{1,0:T(8,128)S(1)}, u32[]{:S(2)}, u32[]{:S(2)}) collective-permute-start(f32[128,128]{1,0:T(8,128)S(1)} %get-tuple-element.73), channel_id=1, source_target_pairs={{0,32},{32,0},{64,96},{96,64},{128,160},{160,128},{192,224},{224,1... | collective-permute-start | bytes 196616 | tf_op jit(solution)/shard_map/ppermute | solution.py:270
  82.9 10.5 %collective-permute-start.24 = (f32[512,128]{1,0:T(8,128)S(1)}, f32[512,128]{1,0:T(8,128)S(1)}, u32[]{:S(2)}, u32[]{:S(2)}) collective-permute-start(f32[512,128]{1,0:T(8,128)S(1)} %collective-permute-done.11), channel_id=1, source_target_pairs={{0,0},{1,1},{2,2},{3,3},{4,4},{5,5},{6,6},{7,7},{8,8},{9,9},{10,10... | collective-permute-start | bytes 786440 | tf_op jit(solution)/shard_map/ppermute | solution.py:279
  83.8 15.4 %collective-permute-start.23 = (f32[512,128]{1,0:T(8,128)S(1)}, f32[512,128]{1,0:T(8,128)S(1)}, u32[]{:S(2)}, u32[]{:S(2)}) collective-permute-start(f32[512,128]{1,0:T(8,128)S(1)} %collective-permute-done.15), channel_id=1, source_target_pairs={{0,0},{1,1},{2,2},{3,3},{4,36},{5,37},{6,38},{7,39},{8,72},{9,73},... | collective-permute-start | bytes 786440 | tf_op jit(solution)/shard_map/ppermute | solution.py:287
  85.7 13.5 %collective-permute-start.22 = (f32[128,128]{1,0:T(8,128)S(1)}, f32[128,128]{1,0:T(8,128)S(1)}, u32[]{:S(2)}, u32[]{:S(2)}) collective-permute-start(f32[128,128]{1,0:T(8,128)S(1)} %add.43.refs_0_), channel_id=1, source_target_pairs={{0,192},{32,224},{64,128},{96,160},{128,64},{160,96},{192,0},{224,... | collective-permute-start | bytes 196616 | tf_op jit(solution)/shard_map/ppermute | solution.py:270
  92.4 6.8 %collective-permute-start.21 = (f32[128,128]{1,0:T(8,128)S(1)}, f32[128,128]{1,0:T(8,128)S(1)}, u32[]{:S(2)}, u32[]{:S(2)}) collective-permute-start(f32[128,128]{1,0:T(8,128)S(1)} %add.43.refs_0_), channel_id=1, source_target_pairs={{0,128},{32,160},{64,192},{96,224},{128,0},{160,32},{192,64},{224,... | collective-permute-start | bytes 196616 | tf_op jit(solution)/shard_map/ppermute | solution.py:270
  92.4 6.8 %collective-permute-start.20 = (f32[128,128]{1,0:T(8,128)S(1)}, f32[128,128]{1,0:T(8,128)S(1)}, u32[]{:S(2)}, u32[]{:S(2)}) collective-permute-start(f32[128,128]{1,0:T(8,128)S(1)} %add.43.refs_0_), channel_id=1, source_target_pairs={{0,64},{32,96},{64,0},{96,32},{128,192},{160,224},{192,128},{224,1... | collective-permute-start | bytes 196616 | tf_op jit(solution)/shard_map/ppermute | solution.py:270
  99.2 15.4 %collective-permute-start.27 = (f32[512,128]{1,0:T(8,128)S(1)}, f32[512,128]{1,0:T(8,128)S(1)}, u32[]{:S(2)}, u32[]{:S(2)}) collective-permute-start(f32[512,128]{1,0:T(8,128)S(1)} %collective-permute-done.23.refs_0_), channel_id=1, source_target_pairs={{0,3},{1,2},{2,1},{3,0},{4,7},{5,6},{6,5},{7,4},{8,11},{9,10},{10,... | collective-permute-start | bytes 786440 | tf_op jit(solution)/shard_map/ppermute | solution.py:274
  102.2 12.4 %collective-permute-start.26 = (f32[512,128]{1,0:T(8,128)S(1)}, f32[512,128]{1,0:T(8,128)S(1)}, u32[]{:S(2)}, u32[]{:S(2)}) collective-permute-start(f32[512,128]{1,0:T(8,128)S(1)} %collective-permute-done.23.refs_0_), channel_id=1, source_target_pairs={{0,2},{1,3},{2,0},{3,1},{4,6},{5,7},{6,4},{7,5},{8,10},{9,11},{10,... | collective-permute-start | bytes 786440 | tf_op jit(solution)/shard_map/ppermute | solution.py:274
  102.8 11.8 %collective-permute-start.25 = (f32[512,128]{1,0:T(8,128)S(1)}, f32[512,128]{1,0:T(8,128)S(1)}, u32[]{:S(2)}, u32[]{:S(2)}) collective-permute-start(f32[512,128]{1,0:T(8,128)S(1)} %collective-permute-done.23.refs_0_), channel_id=1, source_target_pairs={{0,1},{1,0},{2,3},{3,2},{4,5},{5,4},{6,7},{7,6},{8,9},{9,8},{10,11... | collective-permute-start | bytes 786440 | tf_op jit(solution)/shard_map/ppermute | solution.py:274
  117.7 11.0 %copy-start.1 = (f32[2048,512]{1,0:T(8,128)S(1)}, f32[2048,512]{1,0:T(8,128)}, u32[]{:S(2)}) copy-start(f32[2048,512]{1,0:T(8,128)} %refs_4_.3) | copy-start | bytes 12582916
  117.7 1.3 collective-permute-start.28
  119.0 7.6 %collective-permute-start.31 = (f32[128,128]{1,0:T(8,128)S(1)}, f32[128,128]{1,0:T(8,128)S(1)}, u32[]{:S(2)}, u32[]{:S(2)}) collective-permute-start(f32[128,128]{1,0:T(8,128)S(1)} %add.44.refs_0_), channel_id=1, source_target_pairs={{0,192},{32,224},{64,128},{96,160},{128,64},{160,96},{192,0},{224,... | collective-permute-start | bytes 196616 | tf_op jit(solution)/shard_map/ppermute | solution.py:270
  122.6 6.1 %collective-permute-start.30 = (f32[128,128]{1,0:T(8,128)S(1)}, f32[128,128]{1,0:T(8,128)S(1)}, u32[]{:S(2)}, u32[]{:S(2)}) collective-permute-start(f32[128,128]{1,0:T(8,128)S(1)} %add.44.refs_0_), channel_id=1, source_target_pairs={{0,128},{32,160},{64,192},{96,224},{128,0},{160,32},{192,64},{224,... | collective-permute-start | bytes 196616 | tf_op jit(solution)/shard_map/ppermute | solution.py:270
  122.6 6.1 %collective-permute-start.29 = (f32[128,128]{1,0:T(8,128)S(1)}, f32[128,128]{1,0:T(8,128)S(1)}, u32[]{:S(2)}, u32[]{:S(2)}) collective-permute-start(f32[128,128]{1,0:T(8,128)S(1)} %add.44.refs_0_), channel_id=1, source_target_pairs={{0,64},{32,96},{64,0},{96,32},{128,192},{160,224},{192,128},{224,1... | collective-permute-start | bytes 196616 | tf_op jit(solution)/shard_map/ppermute | solution.py:270

commit v2 on v1

--- a/solution.py
+++ b/solution.py
@@ -342,9 +342,9 @@
     edge_turned = turn_row(edge_turned)
     messages = three_rows(mine + swap_row(away, 1))
     panel_cols = lax.dynamic_slice_in_dim(panel_rows, y * cols, cols, 0)
-    panel_cols = turn_row(panel_cols, back=True)
     messages[1], edge_turned, panel_cols = hold(messages[1], edge_turned, panel_cols)
     edges = along_y(edge_turned)
+    panel_cols = turn_row(panel_cols, back=True)
 
     mine = (messages[0] + messages[1]) + (messages[2] + messages[3])
     mine, other = hold(mine, swap_row(mine, 1))
@@ -363,7 +363,7 @@
         in_specs=[scalars()] + whole(3),
         out_specs=whole(5),
     )
-    gram, product_turned, *edges = hold(gram, product_turned, *edges)
+    gram, product_turned, panel_cols, *edges = hold(gram, product_turned, panel_cols, *edges)
 
     gram, product_turned = hold(gram + swap_row(gram, 1), product_turned)
     product_turned = turn_row(product_turned)

time: 136 us -> 135 us (level)
  waiting for transfers between devices: 36.6 us -> 33.5 us
  starting transfers between devices: 56.9 us -> 59.5 us
    ppermute x13, starting transfers between devices: 17.8 us -> 20 us  [swap_row(): return lax.ppermute(x, 'prow', [(r, r ^ mask) for r in range(ROWS)])]
    ppermute x3, waiting for transfers between devices: 6.51 us -> 4.47 us  [turn_row(): return lax.ppermute(x, ('prow', 'pcol'), moves)]
    ppermute x9, waiting for transfers between devices: 8.23 us -> 6.29 us  [swap_y(): return lax.ppermute(x, 'pcol', [(c, c ^ mask) for c in range(ZS * YS)])]
where the time goes in v2:
time: 135 us; the launch traced here: 134 us
  starting transfers between devices  59.5 us (44%)
  Pallas kernels  35.5 us (26%)
  waiting for transfers between devices  33.5 us (25%)
  local copies, waits for them, and re-layouts  4.81 us (4%)
    pallas_call x7, Pallas kernels, block_call(): pl.pallas_call(body, out_shape=[jax.ShapeDtypeStruct(shape, jnp.float32)...  35.5 us
    ppermute x13, starting transfers between devices, swap_row(): return lax.ppermute(x, 'prow', [(r, r ^ mask) for r in range(ROWS)])  20 us
    ppermute x13, waiting for transfers between devices, swap_row(): return lax.ppermute(x, 'prow', [(r, r ^ mask) for r in range(ROWS)])  17.6 us
    ppermute x9, starting transfers between devices, swap_y(): return lax.ppermute(x, 'pcol', [(c, c ^ mask) for c in range(ZS * YS)])  12.5 us
    ppermute x3, starting transfers between devices, turn_row(): return lax.ppermute(x, ('prow', 'pcol'), moves)  8.81 us
    all_to_all x1, starting transfers between devices, on_device(): stack = lax.all_to_all(copies, 'pcol', 0, 0, axis_index_groups=lines)  8.13 us
    ppermute x9, waiting for transfers between devices, swap_y(): return lax.ppermute(x, 'pcol', [(c, c ^ mask) for c in range(ZS * YS)])  6.29 us
    ppermute x3, starting transfers between devices, on_device(): lax.ppermute(pair, 'prow', [(0, 2 * far), (1, 2 * far + 1)])  6.21 us
  transfers between devices with their start and end apart: 33, of which 14 were waited for; matrix products, arithmetic and copies ran while one was open for 0% of the time, Pallas kernels for 19%

profile of v2, /device:TPU:64, one launch (start us, length us, event | category | flops | bytes accessed | tf_op | source)
XLA Modules:
  0.0 134.5 jit_solution(5826937438455951694)
XLA Ops:
  0.6 1.0 slice.9
  1.7 1.5 %broadcast_in_dim.2 = f32[8,64,128]{2,1,0:T(8,128)} broadcast(f32[64,128]{1,0:T(8,128)} %param.3), dimensions={1,2} | broadcast | bytes 294912 | tf_op jit(solution)/shard_map/broadcast_in_dim | solution.py:317
  3.2 1.7 %collective-permute-start.3 = (f32[512,128]{1,0:T(8,128)S(1)}, f32[512,128]{1,0:T(8,128)S(1)}, u32[]{:S(2)}, u32[]{:S(2)}) collective-permute-start(f32[512,128]{1,0:T(8,128)S(1)} %bitcast.13), channel_id=1, source_target_pairs={{0,32},{1,33},{2,34},{3,35},{4,36},{5,37},{6,38},{7,39},{8,40},{9,... | collective-permute-start | bytes 786440 | tf_op jit(solution)/shard_map/ppermute | solution.py:321
  5.0 8.1 %all-to-all-start = ((f32[8,64,128]{2,1,0:T(8,128)}), f32[8,64,128]{2,1,0:T(8,128)S(1)}, u32[]{:S(2)}, u32[]{:S(2)}) async-start(f32[8,64,128]{2,1,0:T(8,128)} %broadcast_in_dim.2), calls=%async_computation | async-start | bytes 524288 | tf_op jit(solution)/shard_map/all_to_all | solution.py:319
  13.1 3.6 %collective-permute-start.6 = (f32[512,128]{1,0:T(8,128)S(1)}, f32[512,128]{1,0:T(8,128)S(1)}, u32[]{:S(2)}, u32[]{:S(2)}) collective-permute-start(f32[512,128]{1,0:T(8,128)S(1)} %broadcast_select_fusion), channel_id=1, source_target_pairs={{0,192},{32,224},{1,193},{33,225},{2,194},{34,226},{3,195},{35,227... | collective-permute-start | bytes 786440 | tf_op jit(solution)/shard_map/ppermute | solution.py:324
  16.7 1.3 collective-permute-start.5
  18.1 1.3 collective-permute-start.4
  19.4 2.4 %all-to-all-done.refs_0_ = f32[8,64,128]{2,1,0:T(8,128)S(1)} async-done(((f32[8,64,128]{2,1,0:T(8,128)}), f32[8,64,128]{2,1,0:T(8,128)S(1)}, u32[]{:S(2)}, u32[]{:S(2)}) %all-to-all-start) | async-done | bytes 262176 | tf_op jit(solution)/shard_map/all_to_all | solution.py:319
  21.7 3.0 %collective-permute-start.2 = (f32[8,64,128]{2,1,0:T(8,128)S(1)}, f32[8,64,128]{2,1,0:T(8,128)S(1)}, u32[]{:S(2)}, u32[]{:S(2)}) collective-permute-start(f32[8,64,128]{2,1,0:T(8,128)S(1)} %all-to-all-done.refs_0_), channel_id=1, source_target_pairs={{0,3},{1,2},{2,1},{3,0},{4,7},{5,6},{6,5},{7,4},{8,11},{9,10},{10,... | collective-permute-start | bytes 786440 | tf_op jit(solution)/shard_map/ppermute | solution.py:274
  24.8 0.6 collective-permute-start.1
  25.9 2.7 %collective-permute-done.4 = f32[512,128]{1,0:T(8,128)S(1)} collective-permute-done((f32[512,128]{1,0:T(8,128)S(1)}, f32[512,128]{1,0:T(8,128)S(1)}, u32[]{:S(2)}, u32[]{:S(2)}) %collective-permute-start.4) | collective-permute-done | bytes 262176 | tf_op jit(solution)/shard_map/ppermute | solution.py:324
  28.7 0.7 collective-permute-start.7
  29.4 3.7 %collective-permute-done.2.refs_3_ = f32[8,64,128]{2,1,0:T(8,128)S(1)} collective-permute-done((f32[8,64,128]{2,1,0:T(8,128)S(1)}, f32[8,64,128]{2,1,0:T(8,128)S(1)}, u32[]{:S(2)}, u32[]{:S(2)}) %collective-permute-start.2) | collective-permute-done | bytes 262176 | tf_op jit(solution)/shard_map/ppermute | solution.py:274
  33.0 0.9 collective-permute-done.1.refs_2_
  34.0 0.5 collective-permute-done.refs_1_
  34.4 2.2 %copy-done = f32[2048,512]{1,0:T(8,128)S(1)} copy-done((f32[2048,512]{1,0:T(8,128)S(1)}, f32[2048,512]{1,0:T(8,128)}, u32[]{:S(2)}) %copy-start) | copy-done | bytes 4194328
  36.6 3.8 %panel.1 = (f32[2048,128]{1,0:T(8,128)S(1)}, f32[384,128]{1,0:T(8,128)S(1)}, f32[384,128]{1,0:T(8,128)S(1)}) custom-call(s32[2]{0:T(128)S(1)} %pad_add_fusion.place_ref, f32[8,64,128]{2,1,0:T(8,128)S(1)} %all-to-all-done.refs_0_, f32[8,64,128]{2,1,0:T(8,128)S(1)} %collective-permute-done.refs_1_, f32[8,64,128]{2,1,0:T(8,128)S(1)} %collective-permute-done.1.refs_2_, ...), custom_call_target="tpu_custom_call" | custom-call | flops 4294967296 | bytes 1048576 | tf_op jit(solution)/shard_map/panel/pallas_call | solution.py:167
  40.9 3.5 %collective-permute-start.10 = (f32[512,128]{1,0:T(8,128)S(1)}, f32[512,128]{1,0:T(8,128)S(1)}, u32[]{:S(2)}, u32[]{:S(2)}) collective-permute-start(f32[512,128]{1,0:T(8,128)S(1)} %collective-permute-done.7), channel_id=1, source_target_pairs={{0,0},{1,1},{2,2},{3,3},{4,36},{5,37},{6,38},{7,39},{8,72},{9,73},... | collective-permute-start | bytes 786440 | tf_op jit(solution)/shard_map/ppermute | solution.py:287
  44.5 2.5 %collective-permute-start.12 = (f32[384,128]{1,0:T(8,128)S(1)}, f32[384,128]{1,0:T(8,128)S(1)}, u32[]{:S(2)}, u32[]{:S(2)}) collective-permute-start(f32[384,128]{1,0:T(8,128)S(1)} %add.36), channel_id=1, source_target_pairs={{0,192},{32,224},{64,128},{96,160},{128,64},{160,96},{192,0},{224,... | collective-permute-start | bytes 589832 | tf_op jit(solution)/shard_map/ppermute | solution.py:270
  47.0 1.6 %collective-permute-start.11 = (f32[384,128]{1,0:T(8,128)S(1)}, f32[384,128]{1,0:T(8,128)S(1)}, u32[]{:S(2)}, u32[]{:S(2)}) collective-permute-start(f32[384,128]{1,0:T(8,128)S(1)} %add.36), channel_id=1, source_target_pairs={{0,128},{32,160},{64,192},{96,224},{128,0},{160,32},{192,64},{224,... | collective-permute-start | bytes 589832 | tf_op jit(solution)/shard_map/ppermute | solution.py:270
  48.6 4.5 %collective-permute-done.10.refs_4_ = f32[512,128]{1,0:T(8,128)S(1)} collective-permute-done((f32[512,128]{1,0:T(8,128)S(1)}, f32[512,128]{1,0:T(8,128)S(1)}, u32[]{:S(2)}, u32[]{:S(2)}) %collective-permute-start.10) | collective-permute-done | bytes 262176 | tf_op jit(solution)/shard_map/ppermute | solution.py:287
  53.1 1.2 collective-permute-done.9
  54.3 7.1 %collective-permute-done.12 = f32[384,128]{1,0:T(8,128)S(1)} collective-permute-done((f32[384,128]{1,0:T(8,128)S(1)}, f32[384,128]{1,0:T(8,128)S(1)}, u32[]{:S(2)}, u32[]{:S(2)}) %collective-permute-start.12) | collective-permute-done | bytes 196640 | tf_op jit(solution)/shard_map/ppermute | solution.py:270
  61.5 3.0 %collective-permute-start.18 = (f32[512,128]{1,0:T(8,128)S(1)}, f32[512,128]{1,0:T(8,128)S(1)}, u32[]{:S(2)}, u32[]{:S(2)}) collective-permute-start(f32[512,128]{1,0:T(8,128)S(1)} %collective-permute-done.10.refs_4_), channel_id=1, source_target_pairs={{0,3},{1,2},{2,1},{3,0},{4,7},{5,6},{6,5},{7,4},{8,11},{9,10},{10,... | collective-permute-start | bytes 786440 | tf_op jit(solution)/shard_map/ppermute | solution.py:274
  64.5 0.7 collective-permute-start.17
  65.2 0.5 collective-permute-start.16
  65.7 1.9 %collective-permute-start.15 = (f32[512,128]{1,0:T(8,128)S(1)}, f32[512,128]{1,0:T(8,128)S(1)}, u32[]{:S(2)}, u32[]{:S(2)}) collective-permute-start(f32[512,128]{1,0:T(8,128)S(1)} %constant_dynamic-slice_fusion), channel_id=1, source_target_pairs={{0,0},{1,1},{2,2},{3,3},{36,4},{37,5},{38,6},{39,7},{72,8},{73,9},... | collective-permute-start | bytes 786440 | tf_op jit(solution)/shard_map/ppermute | solution.py:287
  67.7 0.9 collective-permute-start.14
  68.6 7.9 %first.1 = (f32[128,128]{1,0:T(8,128)}, f32[128,128]{1,0:T(8,128)S(1)}, f32[128,128]{1,0:T(8,128)S(1)}, f32[2048,128]{1,0:T(8,128)S(1)}, f32[128,128]{1,0:T(8,128)S(1)}) custom-call(s32[2]{0:T(128)S(1)} %pad_add_fusion.place_ref, f32[384,128]{1,0:T(8,128)S(1)} %add_add_fusion.mine_ref, f32[384,128]{1,0:T(8,128)S(1)} %collective-permute-done.13.other_ref, ...), custom_call_target="tpu_custom_call" | custom-call | flops 8589934592 | bytes 1048576 | tf_op jit(solution)/shard_map/first/pallas_call | solution.py:167
  76.5 0.6 collective-permute-done.18.refs_7_
  77.1 0.6 collective-permute-done.16.refs_5_
  77.7 6.1 %collective-permute-start.19 = (f32[128,128]{1,0:T(8,128)S(1)}, f32[128,128]{1,0:T(8,128)S(1)}, u32[]{:S(2)}, u32[]{:S(2)}) collective-permute-start(f32[128,128]{1,0:T(8,128)S(1)} %get-tuple-element.75), channel_id=1, source_target_pairs={{0,32},{32,0},{64,96},{96,64},{128,160},{160,128},{192,224},{224,1... | collective-permute-start | bytes 196616 | tf_op jit(solution)/shard_map/ppermute | solution.py:270
  83.8 0.7 collective-permute-start.24
  84.8 3.4 %collective-permute-start.23 = (f32[512,128]{1,0:T(8,128)S(1)}, f32[512,128]{1,0:T(8,128)S(1)}, u32[]{:S(2)}, u32[]{:S(2)}) collective-permute-start(f32[512,128]{1,0:T(8,128)S(1)} %collective-permute-done.14), channel_id=1, source_target_pairs={{0,0},{1,1},{2,2},{3,3},{4,36},{5,37},{6,38},{7,39},{8,72},{9,73},... | collective-permute-start | bytes 786440 | tf_op jit(solution)/shard_map/ppermute | solution.py:287
  88.2 3.6 %collective-permute-start.22 = (f32[128,128]{1,0:T(8,128)S(1)}, f32[128,128]{1,0:T(8,128)S(1)}, u32[]{:S(2)}, u32[]{:S(2)}) collective-permute-start(f32[128,128]{1,0:T(8,128)S(1)} %add.43.refs_0_), channel_id=1, source_target_pairs={{0,192},{32,224},{64,128},{96,160},{128,64},{160,96},{192,0},{224,... | collective-permute-start | bytes 196616 | tf_op jit(solution)/shard_map/ppermute | solution.py:270
  91.8 1.0 collective-permute-start.20
  92.8 7.7 %collective-permute-done.22.refs_3_ = f32[128,128]{1,0:T(8,128)S(1)} collective-permute-done((f32[128,128]{1,0:T(8,128)S(1)}, f32[128,128]{1,0:T(8,128)S(1)}, u32[]{:S(2)}, u32[]{:S(2)}) %collective-permute-start.22) | collective-permute-done | bytes 65568 | tf_op jit(solution)/shard_map/ppermute | solution.py:270
  100.5 3.0 %collective-permute-start.27 = (f32[512,128]{1,0:T(8,128)S(1)}, f32[512,128]{1,0:T(8,128)S(1)}, u32[]{:S(2)}, u32[]{:S(2)}) collective-permute-start(f32[512,128]{1,0:T(8,128)S(1)} %collective-permute-done.23.refs_0_), channel_id=1, source_target_pairs={{0,3},{1,2},{2,1},{3,0},{4,7},{5,6},{6,5},{7,4},{8,11},{9,10},{10,... | collective-permute-start | bytes 786440 | tf_op jit(solution)/shard_map/ppermute | solution.py:274
  103.5 0.6 collective-permute-start.26
  104.2 0.5 collective-permute-start.25
  104.7 4.9 %second.1 = (f32[128,128]{1,0:T(8,128)S(1)}, f32[128,128]{1,0:T(8,128)}, f32[128,128]{1,0:T(8,128)S(1)}, f32[128,128]{1,0:T(8,128)S(1)}) custom-call(f32[128,128]{1,0:T(8,128)S(1)} %add.43.refs_0_, f32[128,128]{1,0:T(8,128)S(1)} %collective-permute-done.20.refs_1_, f32[128,128]{1,0:T(8,128)S(1)} %collective-permute-done.21.refs_2_, ...), custom_call_target="tpu_custom_call" | custom-call | flops 8589934592 | bytes 1048576 | tf_op jit(solution)/shard_map/second/pallas_call | solution.py:167
  109.5 6.4 %third.1 = (f32[128,128]{1,0:T(8,128)}, f32[128,128]{1,0:T(8,128)S(1)}, f32[128,128]{1,0:T(8,128)S(1)}) custom-call(f32[128,128]{1,0:T(8,128)S(1)} %get-tuple-element.86.square_ref), custom_call_target="tpu_custom_call" | custom-call | flops 8589934592 | bytes 1048576 | tf_op jit(solution)/shard_map/third/pallas_call | solution.py:167
  115.9 3.0 %image.1 = (f32[2048,128]{1,0:T(8,128)S(1)}, f32[2048,128]{1,0:T(8,128)S(1)}, f32[128,128]{1,0:T(8,128)S(1)}) custom-call(s32[2]{0:T(128)S(1)} %pad_add_fusion.place_ref, f32[512,128]{1,0:T(8,128)S(1)} %collective-permute-done.23.refs_0_, f32[512,128]{1,0:T(8,128)S(1)} %collective-permute-done.25.refs_1_, f32[512,128]{1,0:T(8,128)S(1)} %collective-permute-done.26.refs_2_, ...), custom_call_target="tpu_custom_call" | custom-call | flops 2147483648 | bytes 1048576 | tf_op jit(solution)/shard_map/image/pallas_call | solution.py:167
  119.1 1.2 collective-permute-done.28
  120.4 1.5 %collective-permute-start.31 = (f32[128,128]{1,0:T(8,128)S(1)}, f32[128,128]{1,0:T(8,128)S(1)}, u32[]{:S(2)}, u32[]{:S(2)}) collective-permute-start(f32[128,128]{1,0:T(8,128)S(1)} %add.44.refs_0_), channel_id=1, source_target_pairs={{0,192},{32,224},{64,128},{96,160},{128,64},{160,96},{192,0},{224,... | collective-permute-start | bytes 196616 | tf_op jit(solution)/shard_map/ppermute | solution.py:270
  121.8 3.0 %collective-permute-start.29 = (f32[128,128]{1,0:T(8,128)S(1)}, f32[128,128]{1,0:T(8,128)S(1)}, u32[]{:S(2)}, u32[]{:S(2)}) collective-permute-start(f32[128,128]{1,0:T(8,128)S(1)} %add.44.refs_0_), channel_id=1, source_target_pairs={{0,64},{32,96},{64,0},{96,32},{128,192},{160,224},{192,128},{224,1... | collective-permute-start | bytes 196616 | tf_op jit(solution)/shard_map/ppermute | solution.py:270
  124.8 3.1 %left.1 = (f32[2048,128]{1,0:T(8,128)S(1)}, f32[2048,128]{1,0:T(8,128)}, f32[512,128]{1,0:T(8,128)S(1)}, f32[512,128]{1,0:T(8,128)S(1)}) custom-call(s32[2]{0:T(128)S(1)} %pad_add_fusion.place_ref, f32[2048,128]{1,0:T(8,128)S(1)} %get-tuple-element.103.base_ref, f32[512,128]{1,0:T(8,128)S(1)} %collective-permute-done.24.panel_ref, f32[512,128]{1,0:T(8,128)S(1)} %bitcast.10, ...), custom_call_target="tpu_custom_call" | custom-call | flops 2147483648 | bytes 1048576 | tf_op jit(solution)/shard_map/left/pallas_call | solution.py:167
  128.1 6.4 %update.1 = f32[2048,512]{1,0:T(8,128)} custom-call(f32[128,128]{1,0:T(8,128)S(1)} %add.44.refs_0_, f32[128,128]{1,0:T(8,128)S(1)} %collective-permute-done.29.refs_1_, f32[128,128]{1,0:T(8,128)S(1)} %collective-permute-done.30.refs_2_, f32[128,128]{1,0:T(8,128)S(1)} %collective-permute-done.31.refs_3_, f32[2048,512]{1,0:T(8,128)S(1)} %copy-done.1, ...), custom_call_target="tpu_custom_call" | custom-call | flops 4294967296 | bytes 1048576 | tf_op jit(solution)/shard_map/update/pallas_call | solution.py:167
  (43 shorter events, 2.0 us)
Async XLA Ops:
  3.2 9.9 %collective-permute-start.3 = (f32[512,128]{1,0:T(8,128)S(1)}, f32[512,128]{1,0:T(8,128)S(1)}, u32[]{:S(2)}, u32[]{:S(2)}) collective-permute-start(f32[512,128]{1,0:T(8,128)S(1)} %bitcast.13), channel_id=1, source_target_pairs={{0,32},{1,33},{2,34},{3,35},{4,36},{5,37},{6,38},{7,39},{8,40},{9,... | collective-permute-start | bytes 786440 | tf_op jit(solution)/shard_map/ppermute | solution.py:321
  5.0 16.8 %all-to-all-start = ((f32[8,64,128]{2,1,0:T(8,128)}), f32[8,64,128]{2,1,0:T(8,128)S(1)}, u32[]{:S(2)}, u32[]{:S(2)}) async-start(f32[8,64,128]{2,1,0:T(8,128)} %broadcast_in_dim.2), calls=%async_computation | async-start | bytes 524288 | tf_op jit(solution)/shard_map/all_to_all | solution.py:319
  13.1 12.3 %collective-permute-start.6 = (f32[512,128]{1,0:T(8,128)S(1)}, f32[512,128]{1,0:T(8,128)S(1)}, u32[]{:S(2)}, u32[]{:S(2)}) collective-permute-start(f32[512,128]{1,0:T(8,128)S(1)} %broadcast_select_fusion), channel_id=1, source_target_pairs={{0,192},{32,224},{1,193},{33,225},{2,194},{34,226},{3,195},{35,227... | collective-permute-start | bytes 786440 | tf_op jit(solution)/shard_map/ppermute | solution.py:324
  16.7 9.2 %collective-permute-start.5 = (f32[512,128]{1,0:T(8,128)S(1)}, f32[512,128]{1,0:T(8,128)S(1)}, u32[]{:S(2)}, u32[]{:S(2)}) collective-permute-start(f32[512,128]{1,0:T(8,128)S(1)} %broadcast_select_fusion), channel_id=1, source_target_pairs={{0,128},{32,160},{1,129},{33,161},{2,130},{34,162},{3,131},{35,163... | collective-permute-start | bytes 786440 | tf_op jit(solution)/shard_map/ppermute | solution.py:324
  18.1 10.6 %collective-permute-start.4 = (f32[512,128]{1,0:T(8,128)S(1)}, f32[512,128]{1,0:T(8,128)S(1)}, u32[]{:S(2)}, u32[]{:S(2)}) collective-permute-start(f32[512,128]{1,0:T(8,128)S(1)} %broadcast_select_fusion), channel_id=1, source_target_pairs={{0,64},{32,96},{1,65},{33,97},{2,66},{34,98},{3,67},{35,99},{4,68}... | collective-permute-start | bytes 786440 | tf_op jit(solution)/shard_map/ppermute | solution.py:324
  21.7 11.3 %collective-permute-start.2 = (f32[8,64,128]{2,1,0:T(8,128)S(1)}, f32[8,64,128]{2,1,0:T(8,128)S(1)}, u32[]{:S(2)}, u32[]{:S(2)}) collective-permute-start(f32[8,64,128]{2,1,0:T(8,128)S(1)} %all-to-all-done.refs_0_), channel_id=1, source_target_pairs={{0,3},{1,2},{2,1},{3,0},{4,7},{5,6},{6,5},{7,4},{8,11},{9,10},{10,... | collective-permute-start | bytes 786440 | tf_op jit(solution)/shard_map/ppermute | solution.py:274
  24.8 9.2 %collective-permute-start.1 = (f32[8,64,128]{2,1,0:T(8,128)S(1)}, f32[8,64,128]{2,1,0:T(8,128)S(1)}, u32[]{:S(2)}, u32[]{:S(2)}) collective-permute-start(f32[8,64,128]{2,1,0:T(8,128)S(1)} %all-to-all-done.refs_0_), channel_id=1, source_target_pairs={{0,2},{1,3},{2,0},{3,1},{4,6},{5,7},{6,4},{7,5},{8,10},{9,11},{10,... | collective-permute-start | bytes 786440 | tf_op jit(solution)/shard_map/ppermute | solution.py:274
  25.4 9.1 %collective-permute-start = (f32[8,64,128]{2,1,0:T(8,128)S(1)}, f32[8,64,128]{2,1,0:T(8,128)S(1)}, u32[]{:S(2)}, u32[]{:S(2)}) collective-permute-start(f32[8,64,128]{2,1,0:T(8,128)S(1)} %all-to-all-done.refs_0_), channel_id=1, source_target_pairs={{0,1},{1,0},{2,3},{3,2},{4,5},{5,4},{6,7},{7,6},{8,9},{9,8},{10,11... | collective-permute-start | bytes 786440 | tf_op jit(solution)/shard_map/ppermute | solution.py:274
  28.7 11.8 %collective-permute-start.7 = (f32[512,128]{1,0:T(8,128)S(1)}, f32[512,128]{1,0:T(8,128)S(1)}, u32[]{:S(2)}, u32[]{:S(2)}) collective-permute-start(f32[512,128]{1,0:T(8,128)S(1)} %add_select_fusion.edge_ref), channel_id=1, source_target_pairs={{0,0},{1,1},{2,2},{3,3},{4,4},{5,5},{6,6},{7,7},{8,8},{9,9},{10,10... | collective-permute-start | bytes 786440 | tf_op jit(solution)/shard_map/ppermute | solution.py:279
  34.4 2.2 %copy-start = (f32[2048,512]{1,0:T(8,128)S(1)}, f32[2048,512]{1,0:T(8,128)}, u32[]{:S(2)}) copy-start(f32[2048,512]{1,0:T(8,128)} %refs_4_.3) | copy-start | bytes 12582916
  40.5 3.9 %collective-permute-start.8 = (f32[384,128]{1,0:T(8,128)S(1)}, f32[384,128]{1,0:T(8,128)S(1)}, u32[]{:S(2)}, u32[]{:S(2)}) collective-permute-start(f32[384,128]{1,0:T(8,128)S(1)} %get-tuple-element.66), channel_id=1, source_target_pairs={{0,32},{32,0},{64,96},{96,64},{128,160},{160,128},{192,224},{224,1... | collective-permute-start | bytes 589832 | tf_op jit(solution)/shard_map/ppermute | solution.py:270
  40.9 12.2 %collective-permute-start.10 = (f32[512,128]{1,0:T(8,128)S(1)}, f32[512,128]{1,0:T(8,128)S(1)}, u32[]{:S(2)}, u32[]{:S(2)}) collective-permute-start(f32[512,128]{1,0:T(8,128)S(1)} %collective-permute-done.7), channel_id=1, source_target_pairs={{0,0},{1,1},{2,2},{3,3},{4,36},{5,37},{6,38},{7,39},{8,72},{9,73},... | collective-permute-start | bytes 786440 | tf_op jit(solution)/shard_map/ppermute | solution.py:287
  44.4 9.8 %collective-permute-start.9 = (f32[384,128]{1,0:T(8,128)S(1)}, f32[384,128]{1,0:T(8,128)S(1)}, u32[]{:S(2)}, u32[]{:S(2)}) collective-permute-start(f32[384,128]{1,0:T(8,128)S(1)} %add.36), channel_id=1, source_target_pairs={{0,64},{32,96},{64,0},{96,32},{128,192},{160,224},{192,128},{224,1... | collective-permute-start | bytes 589832 | tf_op jit(solution)/shard_map/ppermute | solution.py:270
  44.5 16.9 %collective-permute-start.12 = (f32[384,128]{1,0:T(8,128)S(1)}, f32[384,128]{1,0:T(8,128)S(1)}, u32[]{:S(2)}, u32[]{:S(2)}) collective-permute-start(f32[384,128]{1,0:T(8,128)S(1)} %add.36), channel_id=1, source_target_pairs={{0,192},{32,224},{64,128},{96,160},{128,64},{160,96},{192,0},{224,... | collective-permute-start | bytes 589832 | tf_op jit(solution)/shard_map/ppermute | solution.py:270
  47.0 14.4 %collective-permute-start.11 = (f32[384,128]{1,0:T(8,128)S(1)}, f32[384,128]{1,0:T(8,128)S(1)}, u32[]{:S(2)}, u32[]{:S(2)}) collective-permute-start(f32[384,128]{1,0:T(8,128)S(1)} %add.36), channel_id=1, source_target_pairs={{0,128},{32,160},{64,192},{96,224},{128,0},{160,32},{192,64},{224,... | collective-permute-start | bytes 589832 | tf_op jit(solution)/shard_map/ppermute | solution.py:270
  61.4 6.2 %collective-permute-start.13 = (f32[384,128]{1,0:T(8,128)S(1)}, f32[384,128]{1,0:T(8,128)S(1)}, u32[]{:S(2)}, u32[]{:S(2)}) collective-permute-start(f32[384,128]{1,0:T(8,128)S(1)} %add_add_fusion.mine_ref), channel_id=1, source_target_pairs={{0,32},{32,0},{64,96},{96,64},{128,160},{160,128},{192,224},{224,1... | collective-permute-start | bytes 589832 | tf_op jit(solution)/shard_map/ppermute | solution.py:270
  61.5 15.6 %collective-permute-start.18 = (f32[512,128]{1,0:T(8,128)S(1)}, f32[512,128]{1,0:T(8,128)S(1)}, u32[]{:S(2)}, u32[]{:S(2)}) collective-permute-start(f32[512,128]{1,0:T(8,128)S(1)} %collective-permute-done.10.refs_4_), channel_id=1, source_target_pairs={{0,3},{1,2},{2,1},{3,0},{4,7},{5,6},{6,5},{7,4},{8,11},{9,10},{10,... | collective-permute-start | bytes 786440 | tf_op jit(solution)/shard_map/ppermute | solution.py:274
  64.5 12.6 %collective-permute-start.17 = (f32[512,128]{1,0:T(8,128)S(1)}, f32[512,128]{1,0:T(8,128)S(1)}, u32[]{:S(2)}, u32[]{:S(2)}) collective-permute-start(f32[512,128]{1,0:T(8,128)S(1)} %collective-permute-done.10.refs_4_), channel_id=1, source_target_pairs={{0,2},{1,3},{2,0},{3,1},{4,6},{5,7},{6,4},{7,5},{8,10},{9,11},{10,... | collective-permute-start | bytes 786440 | tf_op jit(solution)/shard_map/ppermute | solution.py:274
  65.2 12.5 %collective-permute-start.16 = (f32[512,128]{1,0:T(8,128)S(1)}, f32[512,128]{1,0:T(8,128)S(1)}, u32[]{:S(2)}, u32[]{:S(2)}) collective-permute-start(f32[512,128]{1,0:T(8,128)S(1)} %collective-permute-done.10.refs_4_), channel_id=1, source_target_pairs={{0,1},{1,0},{2,3},{3,2},{4,5},{5,4},{6,7},{7,6},{8,9},{9,8},{10,11... | collective-permute-start | bytes 786440 | tf_op jit(solution)/shard_map/ppermute | solution.py:274
  65.7 10.8 %collective-permute-start.15 = (f32[512,128]{1,0:T(8,128)S(1)}, f32[512,128]{1,0:T(8,128)S(1)}, u32[]{:S(2)}, u32[]{:S(2)}) collective-permute-start(f32[512,128]{1,0:T(8,128)S(1)} %constant_dynamic-slice_fusion), channel_id=1, source_target_pairs={{0,0},{1,1},{2,2},{3,3},{36,4},{37,5},{38,6},{39,7},{72,8},{73,9},... | collective-permute-start | bytes 786440 | tf_op jit(solution)/shard_map/ppermute | solution.py:287
  67.7 10.0 %collective-permute-start.14 = (f32[512,128]{1,0:T(8,128)S(1)}, f32[512,128]{1,0:T(8,128)S(1)}, u32[]{:S(2)}, u32[]{:S(2)}) collective-permute-start(f32[512,128]{1,0:T(8,128)S(1)} %bitcast.9), channel_id=1, source_target_pairs={{0,0},{1,1},{2,2},{3,3},{4,4},{5,5},{6,6},{7,7},{8,8},{9,9},{10,10... | collective-permute-start | bytes 786440 | tf_op jit(solution)/shard_map/ppermute | solution.py:279
  77.7 7.0 %collective-permute-start.19 = (f32[128,128]{1,0:T(8,128)S(1)}, f32[128,128]{1,0:T(8,128)S(1)}, u32[]{:S(2)}, u32[]{:S(2)}) collective-permute-start(f32[128,128]{1,0:T(8,128)S(1)} %get-tuple-element.75), channel_id=1, source_target_pairs={{0,32},{32,0},{64,96},{96,64},{128,160},{160,128},{192,224},{224,1... | collective-permute-start | bytes 196616 | tf_op jit(solution)/shard_map/ppermute | solution.py:270
  83.8 16.6 %collective-permute-start.24 = (f32[512,128]{1,0:T(8,128)S(1)}, f32[512,128]{1,0:T(8,128)S(1)}, u32[]{:S(2)}, u32[]{:S(2)}) collective-permute-start(f32[512,128]{1,0:T(8,128)S(1)} %collective-permute-done.15), channel_id=1, source_target_pairs={{0,0},{1,1},{2,2},{3,3},{4,4},{5,5},{6,6},{7,7},{8,8},{9,9},{10,10... | collective-permute-start | bytes 786440 | tf_op jit(solution)/shard_map/ppermute | solution.py:279
  84.8 15.7 %collective-permute-start.23 = (f32[512,128]{1,0:T(8,128)S(1)}, f32[512,128]{1,0:T(8,128)S(1)}, u32[]{:S(2)}, u32[]{:S(2)}) collective-permute-start(f32[512,128]{1,0:T(8,128)S(1)} %collective-permute-done.14), channel_id=1, source_target_pairs={{0,0},{1,1},{2,2},{3,3},{4,36},{5,37},{6,38},{7,39},{8,72},{9,73},... | collective-permute-start | bytes 786440 | tf_op jit(solution)/shard_map/ppermute | solution.py:287
  88.2 12.3 %collective-permute-start.22 = (f32[128,128]{1,0:T(8,128)S(1)}, f32[128,128]{1,0:T(8,128)S(1)}, u32[]{:S(2)}, u32[]{:S(2)}) collective-permute-start(f32[128,128]{1,0:T(8,128)S(1)} %add.43.refs_0_), channel_id=1, source_target_pairs={{0,192},{32,224},{64,128},{96,160},{128,64},{160,96},{192,0},{224,... | collective-permute-start | bytes 196616 | tf_op jit(solution)/shard_map/ppermute | solution.py:270
  91.8 8.7 %collective-permute-start.21 = (f32[128,128]{1,0:T(8,128)S(1)}, f32[128,128]{1,0:T(8,128)S(1)}, u32[]{:S(2)}, u32[]{:S(2)}) collective-permute-start(f32[128,128]{1,0:T(8,128)S(1)} %add.43.refs_0_), channel_id=1, source_target_pairs={{0,128},{32,160},{64,192},{96,224},{128,0},{160,32},{192,64},{224,... | collective-permute-start | bytes 196616 | tf_op jit(solution)/shard_map/ppermute | solution.py:270
  91.8 8.7 %collective-permute-start.20 = (f32[128,128]{1,0:T(8,128)S(1)}, f32[128,128]{1,0:T(8,128)S(1)}, u32[]{:S(2)}, u32[]{:S(2)}) collective-permute-start(f32[128,128]{1,0:T(8,128)S(1)} %add.43.refs_0_), channel_id=1, source_target_pairs={{0,64},{32,96},{64,0},{96,32},{128,192},{160,224},{192,128},{224,1... | collective-permute-start | bytes 196616 | tf_op jit(solution)/shard_map/ppermute | solution.py:270
  100.5 15.4 %collective-permute-start.27 = (f32[512,128]{1,0:T(8,128)S(1)}, f32[512,128]{1,0:T(8,128)S(1)}, u32[]{:S(2)}, u32[]{:S(2)}) collective-permute-start(f32[512,128]{1,0:T(8,128)S(1)} %collective-permute-done.23.refs_0_), channel_id=1, source_target_pairs={{0,3},{1,2},{2,1},{3,0},{4,7},{5,6},{6,5},{7,4},{8,11},{9,10},{10,... | collective-permute-start | bytes 786440 | tf_op jit(solution)/shard_map/ppermute | solution.py:274
  103.5 12.4 %collective-permute-start.26 = (f32[512,128]{1,0:T(8,128)S(1)}, f32[512,128]{1,0:T(8,128)S(1)}, u32[]{:S(2)}, u32[]{:S(2)}) collective-permute-start(f32[512,128]{1,0:T(8,128)S(1)} %collective-permute-done.23.refs_0_), channel_id=1, source_target_pairs={{0,2},{1,3},{2,0},{3,1},{4,6},{5,7},{6,4},{7,5},{8,10},{9,11},{10,... | collective-permute-start | bytes 786440 | tf_op jit(solution)/shard_map/ppermute | solution.py:274
  104.2 11.8 %collective-permute-start.25 = (f32[512,128]{1,0:T(8,128)S(1)}, f32[512,128]{1,0:T(8,128)S(1)}, u32[]{:S(2)}, u32[]{:S(2)}) collective-permute-start(f32[512,128]{1,0:T(8,128)S(1)} %collective-permute-done.23.refs_0_), channel_id=1, source_target_pairs={{0,1},{1,0},{2,3},{3,2},{4,5},{5,4},{6,7},{7,6},{8,9},{9,8},{10,11... | collective-permute-start | bytes 786440 | tf_op jit(solution)/shard_map/ppermute | solution.py:274
  119.0 9.1 %copy-start.1 = (f32[2048,512]{1,0:T(8,128)S(1)}, f32[2048,512]{1,0:T(8,128)}, u32[]{:S(2)}) copy-start(f32[2048,512]{1,0:T(8,128)} %refs_4_.3) | copy-start | bytes 12582916
  119.0 1.3 collective-permute-start.28
  120.4 7.6 %collective-permute-start.31 = (f32[128,128]{1,0:T(8,128)S(1)}, f32[128,128]{1,0:T(8,128)S(1)}, u32[]{:S(2)}, u32[]{:S(2)}) collective-permute-start(f32[128,128]{1,0:T(8,128)S(1)} %add.44.refs_0_), channel_id=1, source_target_pairs={{0,192},{32,224},{64,128},{96,160},{128,64},{160,96},{192,0},{224,... | collective-permute-start | bytes 196616 | tf_op jit(solution)/shard_map/ppermute | solution.py:270
  121.8 6.1 %collective-permute-start.30 = (f32[128,128]{1,0:T(8,128)S(1)}, f32[128,128]{1,0:T(8,128)S(1)}, u32[]{:S(2)}, u32[]{:S(2)}) collective-permute-start(f32[128,128]{1,0:T(8,128)S(1)} %add.44.refs_0_), channel_id=1, source_target_pairs={{0,128},{32,160},{64,192},{96,224},{128,0},{160,32},{192,64},{224,... | collective-permute-start | bytes 196616 | tf_op jit(solution)/shard_map/ppermute | solution.py:270
  121.8 6.2 %collective-permute-start.29 = (f32[128,128]{1,0:T(8,128)S(1)}, f32[128,128]{1,0:T(8,128)S(1)}, u32[]{:S(2)}, u32[]{:S(2)}) collective-permute-start(f32[128,128]{1,0:T(8,128)S(1)} %add.44.refs_0_), channel_id=1, source_target_pairs={{0,64},{32,96},{64,0},{96,32},{128,192},{160,224},{192,128},{224,1... | collective-permute-start | bytes 196616 | tf_op jit(solution)/shard_map/ppermute | solution.py:270
